TPU v7x, 256 devices: a whole 4x4x8 slice. The times are simulated.
256 devices in a mesh: occ: 32 (over y, x, z_lo), vir: 8 (over z_hi, core).
Axes of the slice: x: 4, y: 4, z: 8 (z_hi: 4, z_lo: 2; z = z_hi * 2 + z_lo), core: 2. Of those that a mesh axis runs over, the one named last changes fastest.
Arguments:
- amplitudes: float32 [2304, 384, 384], P('occ', 'vir'), may hold values from -6 to 6
- integrals: float32 [384, 384, 1536], P('vir', 'occ'), may hold values from -0.015625 to 0.015625
Outputs:
- ladder: float32 [2304, 1536], P('occ', 'vir')
All inputs are finite; a program needn't handle non-finite values.
Results may differ from a plain program's by a relative error of at most 0.000071.
Values sent between devices are 32-bit elements; how exact they have to be, the bound alone decides.
A program may use at most 128 MiB of HBM per device.

v0:
```python
import jax
import jax.numpy as jnp
from jax import lax
from jax.sharding import PartitionSpec as P

O = 48


def on_device(amplitudes, integrals):
    regrouped = lax.all_to_all(amplitudes, "occ", split_axis=2, concat_axis=0, tiled=True)
    pair_count = regrouped.shape[0]
    col_count = regrouped.shape[1] * regrouped.shape[2]
    flattened = regrouped.reshape(pair_count, col_count)
    grouped = flattened.reshape(O, O, col_count)
    summed = (grouped + jnp.transpose(grouped, (1, 0, 2))).reshape(pair_count, col_count)
    slab_matrix = integrals.reshape(col_count, integrals.shape[2])
    pair_share = lax.psum_scatter(
        jnp.dot(
            summed, slab_matrix, precision=lax.Precision.HIGHEST, preferred_element_type=jnp.float32
        ),
        "occ",
        scatter_dimension=0,
        tiled=True,
    )
    finished = lax.psum_scatter(pair_share, "vir", scatter_dimension=1, tiled=True)
    return finished


def solution(mesh):
    in_specs = (P("occ", "vir", None), P("vir", "occ", None))
    out_specs = P("occ", "vir")
    return jax.shard_map(
        on_device, mesh=mesh, in_specs=in_specs, out_specs=out_specs, check_vma=False
    )
```

profile of v0, /device:TPU:32, one launch (start us, length us, event | category | flops | bytes accessed | tf_op | source)
XLA Modules:
  0.0 642.5 jit_solution(9293967096894615325)
XLA Ops:
  6.5 8.4 %copy.13 = f32[72,48,384]{0,1,2:T(8,128)} copy(f32[72,48,384]{2,1,0:T(8,128)} %param.2) | data formatting | bytes 10616832 | tf_op args[0]
  14.9 0.0 copy-start
  14.9 8.9 %all-to-all-start = ((f32[72,48,384]{0,1,2:T(8,128)}), f32[72,48,384]{0,1,2:T(8,128)}, u32[]{:S(2)}, u32[]{:S(2)}) async-start(f32[72,48,384]{0,1,2:T(8,128)} %copy.13), calls=%async_computation | async-start | bytes 18874368 | tf_op jit(solution)/shard_map/all_to_all | solution.py:10
  23.8 0.0 reduce-scatter.5.cloned.1.call-start
  23.8 0.0 copy-done
  23.9 4.3 copy.17
  28.1 3.1 reshape.8
  31.2 136.2 %all-to-all-done = f32[72,48,384]{0,1,2:T(8,128)} async-done(((f32[72,48,384]{0,1,2:T(8,128)}), f32[72,48,384]{0,1,2:T(8,128)}, u32[]{:S(2)}, u32[]{:S(2)}) %all-to-all-start) | async-done | bytes 5308448 | tf_op jit(solution)/shard_map/all_to_all | solution.py:10
  167.4 12.7 %copy.14 = f32[32,72,48,12]{1,0,3,2:T(8,128)} copy(f32[32,72,48,12]{1,2,3,0:T(8,128)} %bitcast.1) | data formatting | bytes 10616832 | tf_op jit(solution)/shard_map/all_to_all | solution.py:10
  180.2 14.9 %reshape_reshape.3 = f32[48,48,576]{1,0,2:T(8,128)} reshape(f32[32,72,48,12]{1,0,3,2:T(8,128)} %copy.14) | data formatting | bytes 10616832 | tf_op jit(solution)/shard_map/reshape;reshape | solution.py:14
  195.1 15.1 %copy.15 = f32[48,48,576]{0,1,2:T(8,128)} copy(f32[48,48,576]{1,0,2:T(8,128)} %reshape_reshape.3) | data formatting | bytes 10616832 | tf_op jit(solution)/shard_map/reshape;reshape | solution.py:14
  210.2 15.2 %bitcast_add_fusion = f32[48,48,576]{1,0,2:T(8,128)} fusion(f32[48,48,576]{1,0,2:T(8,128)} %reshape_reshape.3, f32[48,48,576]{0,1,2:T(8,128)} %copy.15), kind=kLoop, calls=%fused_computation | loop fusion | flops 1327104 | bytes 15925248 | tf_op jit(solution)/shard_map/add | solution.py:15
  225.4 14.0 %copy.16 = f32[48,48,576]{2,1,0:T(8,128)} copy(f32[48,48,576]{1,0,2:T(8,128)} %bitcast_add_fusion) | data formatting | bytes 10616832 | tf_op jit(solution)/shard_map/add | solution.py:15
  239.3 37.5 %fusion = f32[2304,1536]{1,0:T(8,128)} fusion(f32[2304,576]{1,0:T(8,128)} %bitcast.14, f32[576,1536]{1,0:T(8,128)S(1)} %reshape.8), kind=kOutput, calls=%fused_computation.1 | convolution fusion | flops 24461180928 | bytes 23003136 | tf_op jit(solution)/shard_map/dot_general | solution.py:18
  276.8 0.0 reduce-scatter.5.cloned.1.call-update
  276.8 0.0 reduce-scatter.7.cloned.1.call-start
  276.9 316.2 %reduce-scatter.5.cloned.1.call-done = f32[72,1536]{1,0:T(8,128)} async-done(((f32[2304,1536]{1,0:T(8,128)}), f32[72,1536]{1,0:T(8,128)}) %reduce-scatter.5.cloned.1.call-update) | async-done | bytes 442384 | tf_op jit(solution)/shard_map/reduce_scatter | solution.py:17
  593.0 2.2 copy.18
  595.2 0.0 reduce-scatter.7.cloned.1.call-update
  595.2 38.9 %reduce-scatter.7.cloned.1.call-done = f32[192,72]{1,0:T(8,128)} async-done(((f32[1536,72]{1,0:T(8,128)}), f32[192,72]{1,0:T(8,128)}) %reduce-scatter.7.cloned.1.call-update) | async-done | bytes 55312
  634.1 1.6 copy.19
Async XLA Ops:
  14.9 8.9 %copy-start = (f32[48,12,1536]{2,0,1:T(8,128)S(1)}, f32[48,12,1536]{2,0,1:T(8,128)}, u32[]{:S(2)}) copy-start(f32[48,12,1536]{2,0,1:T(8,128)} %param.3) | copy-start | bytes 10616836
  14.9 152.5 %all-to-all-start = ((f32[72,48,384]{0,1,2:T(8,128)}), f32[72,48,384]{0,1,2:T(8,128)}, u32[]{:S(2)}, u32[]{:S(2)}) async-start(f32[72,48,384]{0,1,2:T(8,128)} %copy.13), calls=%async_computation | async-start | bytes 18874368 | tf_op jit(solution)/shard_map/all_to_all | solution.py:10
  23.8 569.2 %reduce-scatter.5.cloned.1.call-start = ((), (), s32[]{:S(2)}) async-start(), calls=%async_computation.3 | async-start | bytes 14598144 | tf_op jit(solution)/shard_map/reduce_scatter | solution.py:17
  276.8 357.3 %reduce-scatter.7.cloned.1.call-start = ((), (), s32[]{:S(2)}) async-start(), calls=%async_computation.4 | async-start | bytes 884736
Sparse Core Ops, SparseCore 0:
  277.0 316.0 reduce-scatter.4
  595.7 38.3 reduce-scatter.6
where the time goes:
time: 645 us; the launch traced here: 643 us
  waiting for transfers between devices  491 us (76%)
  local copies, waits for them, and re-layouts  76.2 us (12%)
  matrix products  37.5 us (6%)
  other arithmetic  15.2 us (2%)
  between operations  13.4 us (2%)
  starting transfers between devices  8.94 us (1%)
    reduce_scatter x1, waiting for transfers between devices, on_device(): lax.psum_scatter(jnp.dot(summed, slab_matrix, precision=lax.Precision.HIG...  316 us
    all_to_all x1, waiting for transfers between devices, on_device(): lax.all_to_all(amplitudes, 'occ', split_axis=2, concat_axis=0, tiled=True)  136 us
    unnamed x3, waiting for transfers between devices  38.9 us
    dot_general x1, matrix products, on_device(): jnp.dot(summed, slab_matrix, precision=lax.Precision.HIGHEST, preferred_e...  37.5 us
    another operation x2, local copies, waits for them, and re-layouts, on_device(): grouped = flattened.reshape(O, O, col_count)  30 us
    unnamed x6, local copies, waits for them, and re-layouts  16.4 us
    add x1, other arithmetic, on_device(): grouped + jnp.transpose(grouped, (1, 0, 2))  15.2 us
    add x1, local copies, waits for them, and re-layouts, on_device(): grouped + jnp.transpose(grouped, (1, 0, 2))  14 us
  transfers between devices with their start and end apart: 3, of which 3 were waited for; matrix products, arithmetic and copies ran while one was open for 1% of the time, Pallas kernels for 0%

commit v1 on v0

v1 whole, which is shorter than its diff:
```python
import functools

import jax
import jax.numpy as jnp
from jax import lax
from jax.experimental import pallas as pl
from jax.experimental.pallas import tpu as pltpu
from jax.sharding import PartitionSpec as P

O = 48
MESH = pl.DeviceIdType.MESH
F32, BF16 = jnp.float32, jnp.bfloat16
SIZE = {"y": 4, "x": 4, "z": 2}
AXIS = {"y": 0, "x": 1, "z": 2}
ORDERS = (("y", "x", "z"), ("x", "z", "y"), ("z", "y", "x"))
ROWS, DEPTH, WIDE, COLS = 72, 576, 640, 1536
PAIRS = 2304


def occ_place():
    r = lax.axis_index("occ")
    return {"y": r // 8, "x": lax.rem(r // 2, 4), "z": lax.rem(r, 2)}


def occ_peer(me, dim, k):
    c = dict(me)
    c[dim] = lax.rem(me[dim] + k, SIZE[dim])
    return c[dim], c["y"] * 8 + c["x"] * 2 + c["z"]


def exchange_kernel(x_ref, o_ref, g1, g2, ssem, rsem, lsem):
    v = lax.axis_index("vir")
    me = occ_place()
    third = ROWS // 3
    barrier = pltpu.get_barrier_semaphore()
    for dim in "yxz":
        for k in range(1, SIZE[dim]):
            pl.semaphore_signal(barrier, inc=1, device_id=(occ_peer(me, dim, k)[1], v), device_id_type=MESH)
    pl.semaphore_wait(barrier, 7)

    def view(ref, t, dim, at, whole):
        ix = [slice(None)] * 3
        ix[AXIS[dim]] = at
        if whole:
            return ref.at[ix[0], ix[1], ix[2], pl.ds(t * third, third)]
        return ref.at[t, ix[0], ix[1], ix[2]]

    held = [(x_ref, True), (g1, False), (g2, False), (o_ref, True)]

    def start(t, s):
        dim = ORDERS[t][s]
        (src, src_whole), (dst, dst_whole) = held[s], held[s + 1]
        copies = []
        for k in range(1, SIZE[dim]):
            at, rank = occ_peer(me, dim, k)
            copies.append(
                pltpu.make_async_remote_copy(
                    src_ref=view(src, t, dim, at, src_whole),
                    dst_ref=view(dst, t, dim, me[dim], dst_whole),
                    send_sem=ssem.at[t, s, k - 1],
                    recv_sem=rsem.at[t, s, k - 1],
                    device_id=(rank, v),
                    device_id_type=MESH,
                )
            )
        copies.append(
            pltpu.make_async_copy(
                view(src, t, dim, me[dim], src_whole), view(dst, t, dim, me[dim], dst_whole), lsem.at[t, s]
            )
        )
        for c in copies:
            c.start()
        return copies

    flying = [start(t, 0) for t in range(3)]
    for s in (1, 2, 3):
        following = []
        for t in range(3):
            for c in flying[t]:
                c.wait()
            if s < 3:
                following.append(start(t, s))
        flying = following


def exchange(x):
    return pl.pallas_call(
        exchange_kernel,
        out_shape=jax.ShapeDtypeStruct((4, 4, 2, ROWS, WIDE), F32),
        in_specs=[pl.BlockSpec(memory_space=pl.ANY)],
        out_specs=pl.BlockSpec(memory_space=pl.ANY),
        scratch_shapes=[
            pltpu.VMEM((3, 4, 4, 2, ROWS // 3, WIDE), F32),
            pltpu.VMEM((3, 4, 4, 2, ROWS // 3, WIDE), F32),
            pltpu.SemaphoreType.DMA((3, 3, 3)),
            pltpu.SemaphoreType.DMA((3, 3, 3)),
            pltpu.SemaphoreType.DMA((3, 3)),
        ],
        compiler_params=pltpu.CompilerParams(collective_id=0, has_side_effects=True, vmem_limit_bytes=40 << 20),
    )(x)


def split(x):
    hi = x.astype(BF16)
    return hi, (x - hi.astype(F32)).astype(BF16)


def product_kernel(a_any, b_ref, c_ref, a_ref, s_hi, s_lo, b_hi, b_lo, sem):
    n = pl.program_id(0)

    @pl.when(n == 0)
    def _():
        tiles = WIDE // 128
        copies = [
            pltpu.make_async_copy(a_any.at[:, pl.ds(t * 128, 128)], a_ref.at[t], sem.at[t]) for t in range(tiles)
        ]
        for c in copies:
            c.start()

        @pl.loop(0, DEPTH // 48)
        def _(k):
            rows = pl.ds(pl.multiple_of(k * 48, 16), 48)
            b = b_ref[rows, :]
            for core in range(2):
                for h in range(2):
                    at = [(2 * h + e) * 384 + core * 192 for e in range(2)]
                    piece = jnp.concatenate([b[:, q : q + 192] for q in at], axis=1)
                    b_hi[core * 2 + h, rows, :], b_lo[core * 2 + h, rows, :] = split(piece)

        for t in range(tiles):
            copies[t].wait()

            @pl.loop(0, O)
            def _(i):
                rows = pl.ds(pl.multiple_of(i * O, 16), O)
                w = min(128, DEPTH - t * 128)
                s = a_ref[t, rows, :] + a_ref[t, pl.ds(i, O, stride=O), :]
                lanes = slice(t * 128, t * 128 + w)
                s_hi[rows, lanes], s_lo[rows, lanes] = split(s[:, :w])

    @pl.loop(0, PAIRS // 256)
    def _(m):
        rows = pl.ds(pl.multiple_of(m * 256, 256), 256)
        dot = functools.partial(jnp.dot, preferred_element_type=F32)
        c_ref[0, rows, :] = (
            dot(s_hi[rows, :], b_lo[n]) + dot(s_lo[rows, :], b_hi[n]) + dot(s_hi[rows, :], b_hi[n])
        )


def product(a, b):
    return pl.pallas_call(
        product_kernel,
        grid=(4,),
        out_shape=jax.ShapeDtypeStruct((4, PAIRS, 384), F32),
        in_specs=[pl.BlockSpec(memory_space=pl.ANY), pl.BlockSpec(memory_space=pltpu.VMEM)],
        out_specs=pl.BlockSpec((1, PAIRS, 384), lambda n: (n, 0, 0)),
        scratch_shapes=[
            pltpu.VMEM((WIDE // 128, PAIRS, 128), F32),
            pltpu.VMEM((PAIRS, DEPTH), BF16),
            pltpu.VMEM((PAIRS, DEPTH), BF16),
            pltpu.VMEM((4, DEPTH, 384), BF16),
            pltpu.VMEM((4, DEPTH, 384), BF16),
            pltpu.SemaphoreType.DMA((WIDE // 128,)),
        ],
        compiler_params=pltpu.CompilerParams(vmem_limit_bytes=48 << 20),
        cost_estimate=pl.CostEstimate(flops=6 * PAIRS * DEPTH * COLS, bytes_accessed=24 << 20, transcendentals=0),
    )(a, b)


def reduce_kernel(c_ref, o_ref, acc, other, r1, s1, r2, s2, r3, ssem, rsem, lsem):
    v = lax.axis_index("vir")
    core, zh = lax.rem(v, 2), v // 2
    me = occ_place()
    r = lax.axis_index("occ")
    zl = me["z"]
    barrier = pltpu.get_barrier_semaphore()

    def line(k):
        z = lax.rem(zh * 2 + zl + k, 8)
        zl_to, zh_to = lax.rem(z, 2), z // 2
        return zl_to, zh_to, (r - zl + zl_to, zh_to * 2 + core)

    twin = (r, v + 1 - 2 * core)
    devices = [twin] + [(occ_peer(me, dim, k)[1], v) for dim in "yx" for k in range(1, 4)]
    devices += [line(k)[2] for k in range(1, 8)]
    for d in devices:
        pl.semaphore_signal(barrier, inc=1, device_id=d, device_id_type=MESH)
    pl.semaphore_wait(barrier, len(devices))

    def remote(n, src, dst, device):
        c = pltpu.make_async_remote_copy(
            src_ref=src, dst_ref=dst, send_sem=ssem.at[n], recv_sem=rsem.at[n], device_id=device, device_id_type=MESH
        )
        c.start()
        return c

    own = [pltpu.make_async_copy(c_ref.at[core * 2 + h], acc.at[h], lsem.at[h]) for h in range(2)]
    for c in own:
        c.start()
    swap = [remote(h, c_ref.at[(1 - core) * 2 + h], other.at[h], twin) for h in range(2)]
    first = []
    for h in range(2):
        own[h].wait()
        swap[h].wait()

        @pl.loop(0, PAIRS // 72)
        def _(m):
            rows = pl.ds(pl.multiple_of(m * 72, 8), 72)
            acc[h, rows, :] += other[h, rows, :]

        dim = "yx"[h]
        for k in range(1, 4):
            at, rank = occ_peer(me, dim, k)
            rows = pl.ds(pl.multiple_of(at * 576, 8), 576)
            if h == 0:
                first.append(remote(2 + k - 1, acc.at[0, rows], r1.at[0, k - 1], (rank, v)))
            else:
                for y in range(4):
                    rows = pl.ds(pl.multiple_of(y * 576 + at * 144, 8), 144)
                    first.append(
                        remote(5 + (k - 1) * 4 + y, acc.at[1, rows], r1.at[1, k - 1, pl.ds(y * 144, 144)], (rank, v))
                    )

    second = []
    for h in range(2):
        for c in first[:3] if h == 0 else first[3:]:
            c.wait()
        for y in range(4):
            part = pl.ds(y * 144, 144)
            base = (me["y"] * 576 + y * 144) if h == 0 else (y * 576 + me["x"] * 144)
            mine = pl.ds(pl.multiple_of(base, 8), 144)
            s1[h, part, :] = (acc[h, mine, :] + r1[h, 0, part, :]) + (r1[h, 1, part, :] + r1[h, 2, part, :])
        dim = "xy"[h]
        for k in range(1, 4):
            at, rank = occ_peer(me, dim, k)
            rows = pl.ds(pl.multiple_of(at * 144, 8), 144)
            second.append(remote(17 + h * 3 + k - 1, s1.at[h, rows], r2.at[h, k - 1], (rank, v)))

    for h in range(2):
        for c in second[3 * h : 3 * h + 3]:
            c.wait()
        mine = pl.ds(pl.multiple_of(me["xy"[h]] * 144, 8), 144)
        s2[h] = (s1[h, mine, :] + r2[h, 0]) + (r2[h, 1] + r2[h, 2])

    def part(zl_to, zh_to):
        rows = pl.ds(pl.multiple_of(zl_to * 72, 8), 72)
        lanes = pl.ds(pl.multiple_of(lax.rem(zh_to, 2) * 128, 128), 256)
        return s2.at[zh_to // 2, rows, lanes]

    third = []
    for k in range(1, 8):
        zl_to, zh_to, device = line(k)
        third.append(remote(23 + k - 1, part(zl_to, zh_to), r3.at[k - 1], device))
    total = part(zl, zh)[...]
    for k in range(1, 8):
        third[k - 1].wait()
        total += r3[k - 1]
    o_ref[...] = jnp.where(lax.rem(zh, 2) == 0, total[:, :192], total[:, 64:])


def reduce(c):
    return pl.pallas_call(
        reduce_kernel,
        out_shape=jax.ShapeDtypeStruct((ROWS, 192), F32),
        in_specs=[pl.BlockSpec(memory_space=pl.ANY)],
        out_specs=pl.BlockSpec(memory_space=pltpu.VMEM),
        scratch_shapes=[
            pltpu.VMEM((2, PAIRS, 384), F32),
            pltpu.VMEM((2, PAIRS, 384), F32),
            pltpu.VMEM((2, 3, 576, 384), F32),
            pltpu.VMEM((2, 576, 384), F32),
            pltpu.VMEM((2, 3, 144, 384), F32),
            pltpu.VMEM((2, 144, 384), F32),
            pltpu.VMEM((7, ROWS, 256), F32),
            pltpu.SemaphoreType.DMA((30,)),
            pltpu.SemaphoreType.DMA((30,)),
            pltpu.SemaphoreType.DMA((2,)),
        ],
        compiler_params=pltpu.CompilerParams(collective_id=1, has_side_effects=True, vmem_limit_bytes=48 << 20),
    )(c)


def on_device(amplitudes, integrals):
    slabs = amplitudes.reshape(ROWS, O, 32, 12).transpose(2, 0, 3, 1).reshape(4, 4, 2, ROWS, DEPTH)
    slabs = jnp.pad(slabs, ((0, 0),) * 4 + ((0, WIDE - DEPTH),))
    columns = exchange(slabs).reshape(PAIRS, WIDE)
    slab_matrix = integrals.transpose(1, 0, 2).reshape(DEPTH, COLS)
    return reduce(product(columns, slab_matrix))


def solution(mesh):
    in_specs = (P("occ", "vir", None), P("vir", "occ", None))
    out_specs = P("occ", "vir")
    return jax.shard_map(
        on_device, mesh=mesh, in_specs=in_specs, out_specs=out_specs, check_vma=False
    )
```

time: 645 us -> 220 us (0.34)
  waiting for transfers between devices: 491 us -> 0 us
  Pallas kernels: 0 us -> 194 us
  local copies, waits for them, and re-layouts: 76.2 us -> 24.3 us
  matrix products: 37.5 us -> 0 us
  other arithmetic: 15.2 us -> 0 us
  between operations: 13.4 us -> 0.05 us
  starting transfers between devices: 8.94 us -> 0 us
    reduce_scatter x1 -> x0, waiting for transfers between devices: 316 us -> none  [on_device(): lax.psum_scatter(jnp.dot(summed, slab_matrix, precision=lax.Precision.HIG...]
    pallas_call x0 -> x3, Pallas kernels: none -> 194 us  [the longest x1 84.7 us: reduce(): pl.pallas_call(reduce_kernel, out_shape=jax.ShapeDtypeStruct((ROWS, 192),...]
    all_to_all x1 -> x0, waiting for transfers between devices: 136 us -> none  [on_device(): lax.all_to_all(amplitudes, 'occ', split_axis=2, concat_axis=0, tiled=True)]
    unnamed x3 -> x0, waiting for transfers between devices: 38.9 us -> none
    dot_general x1 -> x0, matrix products: 37.5 us -> none  [on_device(): jnp.dot(summed, slab_matrix, precision=lax.Precision.HIGHEST, preferred_e...]
    another operation x2 -> x0, local copies, waits for them, and re-layouts: 30 us -> none  [on_device(): grouped = flattened.reshape(O, O, col_count)]
    add x1 -> x0, other arithmetic: 15.2 us -> none  [on_device(): grouped + jnp.transpose(grouped, (1, 0, 2))]
    add x1 -> x0, local copies, waits for them, and re-layouts: 14 us -> none  [on_device(): grouped + jnp.transpose(grouped, (1, 0, 2))]
  transfers between devices with their start and end apart: 3 -> 0, of which waited for: 3 -> 0; matrix products, arithmetic and copies ran while one was open for 1% -> 0% of each run, Pallas kernels for 0% -> 0%
where the time goes in v1:
time: 220 us; the launch traced here: 219 us
  Pallas kernels  194 us (88%)
  local copies, waits for them, and re-layouts  24.3 us (11%)
    pallas_call x1, Pallas kernels, reduce(): pl.pallas_call(reduce_kernel, out_shape=jax.ShapeDtypeStruct((ROWS, 192),...  84.7 us
    pallas_call x1, Pallas kernels, exchange(): pl.pallas_call(exchange_kernel, out_shape=jax.ShapeDtypeStruct((4, 4, 2,...  75.1 us
    pallas_call x1, Pallas kernels, product(): pl.pallas_call(product_kernel, grid=(4,), out_shape=jax.ShapeDtypeStruct(...  34.4 us
    unnamed x6, local copies, waits for them, and re-layouts  11.5 us
    reshape x1, local copies, waits for them, and re-layouts, on_device(): amplitudes.reshape(ROWS, O, 32, 12).transpose(2, 0, 3, 1)  9.59 us

profile of v1, /device:TPU:32, one launch (start us, length us, event | category | flops | bytes accessed | tf_op | source)
XLA Modules:
  0.0 218.7 jit_solution(16648069697904776797)
XLA Ops:
  0.0 8.5 %copy.4 = f32[72,48,384]{0,1,2:T(8,128)} copy(f32[72,48,384]{2,1,0:T(8,128)} %param.2) | data formatting | bytes 10616832 | tf_op args[0]
  8.5 9.6 %copy.5 = f32[4,4,2,72,576]{4,3,2,1,0:T(8,128)} copy(f32[4,4,2,72,576]{3,4,2,1,0:T(8,128)} %bitcast.11) | data formatting | bytes 10616832 | tf_op jit(solution)/shard_map/reshape | solution.py:284
  18.0 3.2 %pad.4.x_ref = f32[4,4,2,72,640]{4,3,2,1,0:T(8,128)S(1)} pad(f32[4,4,2,72,576]{4,3,2,1,0:T(8,128)} %copy.5, f32[]{:T(128)} %constant.2.clone.1), padding=0_0x0_0x0_0x0_0x0_64 | pad | bytes 11206660 | tf_op jit(solution)/shard_map/jit(_pad)/pad | solution.py:285
  21.2 0.0 copy-start.1
  21.3 75.1 %shard_map.28 = f32[4,4,2,72,640]{4,3,2,1,0:T(8,128)S(1)} custom-call(f32[4,4,2,72,640]{4,3,2,1,0:T(8,128)S(1)} %pad.4.x_ref), custom_call_target="tpu_custom_call" | custom-call | tf_op jit(solution)/shard_map/pallas_call | solution.py:87
  96.4 0.0 copy-start
  96.4 2.4 %copy-done = f32[4,4,2,72,640]{4,3,2,1,0:T(8,128)} copy-done((f32[4,4,2,72,640]{4,3,2,1,0:T(8,128)}, f32[4,4,2,72,640]{4,3,2,1,0:T(8,128)S(1)}, u32[]{:S(2)}) %copy-start) | copy-done | bytes 5898264
  98.8 0.0 copy-done.1
  98.8 34.4 %shard_map.29.c_ref = f32[4,2304,384]{2,1,0:T(8,128)} custom-call(f32[2304,640]{1,0:T(8,128)} %bitcast.9, f32[576,1536]{1,0:T(8,128)S(1)} %bitcast.10), custom_call_target="tpu_custom_call" | custom-call | flops 12230590464 | bytes 25165824 | tf_op jit(solution)/shard_map/pallas_call | solution.py:151
  133.3 84.7 %shard_map.30 = f32[72,192]{1,0:T(8,128)S(1)} custom-call(f32[4,2304,384]{2,1,0:T(8,128)} %shard_map.29.c_ref), custom_call_target="tpu_custom_call" | custom-call | tf_op jit(solution)/shard_map/pallas_call | solution.py:262
  218.0 0.6 copy.7
Async XLA Ops:
  21.2 77.6 %copy-start.1 = (f32[48,12,1536]{2,0,1:T(8,128)S(1)}, f32[48,12,1536]{2,0,1:T(8,128)}, u32[]{:S(2)}) copy-start(f32[48,12,1536]{2,0,1:T(8,128)} %param.3) | copy-start | bytes 10616836
  96.4 2.5 %copy-start = (f32[4,4,2,72,640]{4,3,2,1,0:T(8,128)}, f32[4,4,2,72,640]{4,3,2,1,0:T(8,128)S(1)}, u32[]{:S(2)}) copy-start(f32[4,4,2,72,640]{4,3,2,1,0:T(8,128)S(1)} %shard_map.28) | copy-start | bytes 17694724

commit v2 on v1

v2 whole, which is shorter than its diff:
```python
import functools

import jax
import jax.numpy as jnp
from jax import lax
from jax.experimental import pallas as pl
from jax.experimental.pallas import tpu as pltpu
from jax.sharding import PartitionSpec as P

O = 48
MESH = pl.DeviceIdType.MESH
F32, BF16 = jnp.float32, jnp.bfloat16
SIZE = {"y": 4, "x": 4, "z": 2}
AXIS = {"y": 0, "x": 1, "z": 2}
ORDERS = (("y", "x", "z"), ("x", "z", "y"), ("z", "y", "x"))
ROWS, DEPTH, WIDE, COLS = 72, 576, 640, 1536
PAIRS = 2304


def occ_place():
    r = lax.axis_index("occ")
    return {"y": r // 8, "x": lax.rem(r // 2, 4), "z": lax.rem(r, 2)}


def occ_peer(me, dim, k):
    c = dict(me)
    c[dim] = lax.rem(me[dim] + k, SIZE[dim])
    return c[dim], c["y"] * 8 + c["x"] * 2 + c["z"]


def exchange_kernel(x_ref, o_ref, g1, g2, ssem, rsem, lsem):
    v = lax.axis_index("vir")
    me = occ_place()
    third = ROWS // 3
    barrier = pltpu.get_barrier_semaphore()
    for dim in "yxz":
        for k in range(1, SIZE[dim]):
            pl.semaphore_signal(barrier, inc=1, device_id=(occ_peer(me, dim, k)[1], v), device_id_type=MESH)
    pl.semaphore_wait(barrier, 7)

    def view(ref, t, dim, at, whole):
        ix = [slice(None)] * 3
        ix[AXIS[dim]] = at
        if whole:
            return ref.at[ix[0], ix[1], ix[2], pl.ds(t * third, third)]
        return ref.at[t, ix[0], ix[1], ix[2]]

    held = [(x_ref, True), (g1, False), (g2, False), (o_ref, True)]

    def start(t, s):
        dim = ORDERS[t][s]
        (src, src_whole), (dst, dst_whole) = held[s], held[s + 1]
        copies = []
        for k in range(1, SIZE[dim]):
            at, rank = occ_peer(me, dim, k)
            copies.append(
                pltpu.make_async_remote_copy(
                    src_ref=view(src, t, dim, at, src_whole),
                    dst_ref=view(dst, t, dim, me[dim], dst_whole),
                    send_sem=ssem.at[t, s, k - 1],
                    recv_sem=rsem.at[t, s, k - 1],
                    device_id=(rank, v),
                    device_id_type=MESH,
                )
            )
        copies.append(
            pltpu.make_async_copy(
                view(src, t, dim, me[dim], src_whole), view(dst, t, dim, me[dim], dst_whole), lsem.at[t, s]
            )
        )
        for c in copies:
            c.start()
        return copies

    flying = [start(t, 0) for t in range(3)]
    for s in (1, 2, 3):
        following = []
        for t in range(3):
            for c in flying[t]:
                c.wait()
            if s < 3:
                following.append(start(t, s))
        flying = following


def exchange(x):
    return pl.pallas_call(
        exchange_kernel,
        out_shape=jax.ShapeDtypeStruct((4, 4, 2, ROWS, WIDE), F32),
        in_specs=[pl.BlockSpec(memory_space=pl.ANY)],
        out_specs=pl.BlockSpec(memory_space=pl.ANY),
        scratch_shapes=[
            pltpu.VMEM((3, 4, 4, 2, ROWS // 3, WIDE), F32),
            pltpu.VMEM((3, 4, 4, 2, ROWS // 3, WIDE), F32),
            pltpu.SemaphoreType.DMA((3, 3, 3)),
            pltpu.SemaphoreType.DMA((3, 3, 3)),
            pltpu.SemaphoreType.DMA((3, 3)),
        ],
        compiler_params=pltpu.CompilerParams(collective_id=0, has_side_effects=True, vmem_limit_bytes=40 << 20),
    )(x)


def split(x):
    hi = x.astype(BF16)
    return hi, (x - hi.astype(F32)).astype(BF16)


TURN = (2, 0, 1)
KEPT = 80
UNIQUE = 16 * KEPT


def runs(start, count, *stops):
    out = []
    while count:
        start %= O
        n = min([count, O - start] + [p - start for p in stops if p > start])
        out.append((start, n))
        start, count = start + n, count - n
    return out


def pair_sum_kernel(a_any, hi_ref, lo_ref, a_ref, sem):
    tiles = WIDE // 128
    copies = [pltpu.make_async_copy(a_any.at[:, pl.ds(t * 128, 128)], a_ref.at[t], sem.at[t]) for t in range(tiles)]
    for c in copies:
        c.start()
    for t in range(tiles):
        copies[t].wait()
        for q in range(16):
            rows = []
            for k in range(3):
                i, m = 3 * q + TURN[k], int(k == 0)
                rows += [
                    a_ref[t, i * O + j : i * O + j + n, :] + a_ref[t, pl.ds(j * O + i, n, stride=O), :]
                    for j, n in runs(3 * q + m, 27 - m)
                ]
            at, lanes = slice(q * KEPT, (q + 1) * KEPT), slice(t * 128, (t + 1) * 128)
            hi_ref[at, lanes], lo_ref[at, lanes] = split(jnp.concatenate(rows, axis=0))


def pair_sum(a):
    return pl.pallas_call(
        pair_sum_kernel,
        out_shape=[jax.ShapeDtypeStruct((UNIQUE, WIDE), BF16)] * 2,
        in_specs=[pl.BlockSpec(memory_space=pl.ANY)],
        out_specs=[pl.BlockSpec(memory_space=pltpu.VMEM)] * 2,
        scratch_shapes=[
            pltpu.VMEM((WIDE // 128, PAIRS, 128), F32),
            pltpu.SemaphoreType.DMA((WIDE // 128,)),
        ],
        compiler_params=pltpu.CompilerParams(vmem_limit_bytes=24 << 20),
    )(a)


def ladder_kernel(
    hi_ref, lo_ref, b_ref, o_ref, b_hi, b_lo, away, acc, other, r1, s1, r2, s2, r3, mine, r4, ends, r5, ssem, rsem
):
    v = lax.axis_index("vir")
    core, zh = lax.rem(v, 2), v // 2
    me = occ_place()
    r = lax.axis_index("occ")
    q, zl = r // 2, me["z"]
    barrier = pltpu.get_barrier_semaphore()

    def triple(k):
        return (lax.rem(q + k, 16) * 2 + zl, v)

    def high(k):
        to = lax.rem(zh + k, 4)
        return to, (r, to * 2 + core)

    twin = (r, v + 1 - 2 * core)
    beside = (r + 1 - 2 * zl, v)
    devices = [twin, beside] + [triple(k) for k in range(1, 16)] + [high(k)[1] for k in range(1, 4)]
    for d in devices:
        pl.semaphore_signal(barrier, inc=1, device_id=d, device_id_type=MESH)

    sent = [0]

    def remote(src, dst, device):
        n = sent[0]
        sent[0] += 1
        c = pltpu.make_async_remote_copy(
            src_ref=src, dst_ref=dst, send_sem=ssem.at[n], recv_sem=rsem.at[n], device_id=device, device_id_type=MESH
        )
        c.start()
        return c

    @pl.loop(0, DEPTH // 48)
    def _(k):
        rows = pl.ds(pl.multiple_of(k * 48, 16), 48)
        b = b_ref[rows, :]
        for c in range(2):
            for h in range(2):
                at = [(2 * h + e) * 384 + c * 192 for e in range(2)]
                piece = jnp.concatenate([b[:, p : p + 192] for p in at], axis=1)
                b_hi[c * 2 + h, rows, :], b_lo[c * 2 + h, rows, :] = split(piece)

    def product(n, out, h):
        @pl.loop(0, UNIQUE // 256)
        def _(m):
            rows = pl.ds(pl.multiple_of(m * 256, 256), 256)
            dot = functools.partial(jnp.dot, preferred_element_type=F32)
            hi, lo = hi_ref[rows, :DEPTH], lo_ref[rows, :DEPTH]
            out[h, rows, :] = dot(hi, b_lo[n]) + dot(lo, b_hi[n]) + dot(hi, b_hi[n])

    swap = []
    for h in range(2):
        product((1 - core) * 2 + h, away, h)
        if h == 0:
            pl.semaphore_wait(barrier, len(devices))
        swap.append(remote(away.at[h], other.at[h], twin))

    first = [[], []]
    for h in range(2):
        product(core * 2 + h, acc, h)
        swap[h].wait()

        @pl.loop(0, 16)
        def _(m):
            rows = pl.ds(pl.multiple_of(m * KEPT, 8), KEPT)
            acc[h, rows, :] += other[h, rows, :]

        dim = "yx"[h]
        for k in range(1, 4):
            at, rank = occ_peer(me, dim, k)
            if h == 0:
                rows = pl.ds(pl.multiple_of(at * 4 * KEPT, 8), 4 * KEPT)
                first[h].append(remote(acc.at[h, rows], r1.at[h, k - 1], (rank, v)))
            else:
                for y in range(4):
                    rows = pl.ds(pl.multiple_of((y * 4 + at) * KEPT, 8), KEPT)
                    first[h].append(remote(acc.at[h, rows], r1.at[h, k - 1, pl.ds(y * KEPT, KEPT)], (rank, v)))

    second = [[], []]
    for h in range(2):
        for c in first[h]:
            c.wait()
        for y in range(4):
            part = pl.ds(y * KEPT, KEPT)
            base = (me["y"] * 4 + y) if h == 0 else (y * 4 + me["x"])
            own = pl.ds(pl.multiple_of(base * KEPT, 8), KEPT)
            s1[h, part, :] = (acc[h, own, :] + r1[h, 0, part, :]) + (r1[h, 1, part, :] + r1[h, 2, part, :])
        for k in range(1, 4):
            at, rank = occ_peer(me, "xy"[h], k)
            rows = pl.ds(pl.multiple_of(at * KEPT, 8), KEPT)
            second[h].append(remote(s1.at[h, rows], r2.at[h, k - 1], (rank, v)))

    for h in range(2):
        for c in second[h]:
            c.wait()
        own = pl.ds(pl.multiple_of(me["xy"[h]] * KEPT, 8), KEPT)
        s2[h] = (s1[h, own, :] + r2[h, 0]) + (r2[h, 1] + r2[h, 2])

    def part(to):
        return s2.at[to // 2, :, pl.ds(pl.multiple_of(lax.rem(to, 2) * 128, 128), 256)]

    third = [remote(part(high(k)[0]), r3.at[k - 1], high(k)[1]) for k in range(1, 4)]
    total = part(zh)[...]
    for k in range(1, 4):
        third[k - 1].wait()
        total += r3[k - 1]
    mine[...] = jnp.where(lax.rem(zh, 2) == 0, total[:, :192], total[:, 64:])
    fourth = remote(mine, r4, beside)
    fourth.wait()
    u = mine[...] + r4[...]

    def kept(k, m):
        return u[27 * k - 1 + m : 27 * k + m]

    fifth = []
    for k in range(1, 8):
        ends[k - 1, :9] = jnp.concatenate([kept(e, 3 * k + t) for t in range(3) for e in (1, 2, 0)], axis=0)
        fifth.append(remote(ends.at[k - 1], r5.at[k - 1], triple(k)))
    for c in fifth:
        c.wait()
    turned = []
    for t in range(3):
        k = TURN.index(t)
        rows = [u[27 * k - 1 : 27 * k + 26]] if k else [kept(1, 2), u[0:26]]
        rows += [r5[6 - e, 3 * t : 3 * t + 3] for e in range(7)]
        turned.append(pltpu.roll(jnp.concatenate(rows, axis=0), 3 * q, 0))
    low = jnp.concatenate([turned[0], turned[1][:24]], axis=0)
    top = jnp.concatenate([turned[1][24:], turned[2]], axis=0)
    o_ref[...] = jnp.where(zl == 0, low, top)


def ladder(hi, lo, b):
    return pl.pallas_call(
        ladder_kernel,
        out_shape=jax.ShapeDtypeStruct((ROWS, 192), F32),
        in_specs=[pl.BlockSpec(memory_space=pltpu.VMEM)] * 3,
        out_specs=pl.BlockSpec(memory_space=pltpu.VMEM),
        scratch_shapes=[
            pltpu.VMEM((4, DEPTH, 384), BF16),
            pltpu.VMEM((4, DEPTH, 384), BF16),
            pltpu.VMEM((2, UNIQUE, 384), F32),
            pltpu.VMEM((2, UNIQUE, 384), F32),
            pltpu.VMEM((2, UNIQUE, 384), F32),
            pltpu.VMEM((2, 3, 4 * KEPT, 384), F32),
            pltpu.VMEM((2, 4 * KEPT, 384), F32),
            pltpu.VMEM((2, 3, KEPT, 384), F32),
            pltpu.VMEM((2, KEPT, 384), F32),
            pltpu.VMEM((3, KEPT, 256), F32),
            pltpu.VMEM((KEPT, 192), F32),
            pltpu.VMEM((KEPT, 192), F32),
            pltpu.VMEM((7, 16, 192), F32),
            pltpu.VMEM((7, 16, 192), F32),
            pltpu.SemaphoreType.DMA((34,)),
            pltpu.SemaphoreType.DMA((34,)),
        ],
        compiler_params=pltpu.CompilerParams(collective_id=1, has_side_effects=True, vmem_limit_bytes=48 << 20),
    )(hi, lo, b)


def on_device(amplitudes, integrals):
    slabs = amplitudes.reshape(ROWS, O, 32, 12).transpose(2, 0, 3, 1).reshape(4, 4, 2, ROWS, DEPTH)
    slabs = jnp.pad(slabs, ((0, 0),) * 4 + ((0, WIDE - DEPTH),))
    columns = exchange(slabs).reshape(PAIRS, WIDE)
    slab_matrix = integrals.transpose(1, 0, 2).reshape(DEPTH, COLS)
    return ladder(*pair_sum(columns), slab_matrix)


def solution(mesh):
    in_specs = (P("occ", "vir", None), P("vir", "occ", None))
    out_specs = P("occ", "vir")
    return jax.shard_map(
        on_device, mesh=mesh, in_specs=in_specs, out_specs=out_specs, check_vma=False
    )
```

time: 220 us -> 170 us (0.77)
  Pallas kernels: 194 us -> 148 us
  local copies, waits for them, and re-layouts: 24.3 us -> 21.9 us
    pallas_call x2, Pallas kernels: 119 us -> 72.5 us  [the longest x1 70.7 us: ladder(): pl.pallas_call(ladder_kernel, out_shape=jax.ShapeDtypeStruct((ROWS, 192),...]
    unnamed x6 -> x2, local copies, waits for them, and re-layouts: 11.5 us -> 9.07 us
where the time goes in v2:
time: 170 us
  Pallas kernels  148 us (87%)
  local copies, waits for them, and re-layouts  21.9 us (13%)
    pallas_call x1, Pallas kernels, exchange(): pl.pallas_call(exchange_kernel, out_shape=jax.ShapeDtypeStruct((4, 4, 2,...  75.1 us
    pallas_call x1, Pallas kernels, ladder(): pl.pallas_call(ladder_kernel, out_shape=jax.ShapeDtypeStruct((ROWS, 192),...  70.7 us
    reshape x1, local copies, waits for them, and re-layouts, on_device(): amplitudes.reshape(ROWS, O, 32, 12).transpose(2, 0, 3, 1)  9.59 us
    unnamed x2, local copies, waits for them, and re-layouts  9.07 us

profile of v2, /device:TPU:32, one launch (start us, length us, event | category | flops | bytes accessed | tf_op | source)
XLA Modules:
  0.0 169.6 jit_solution(9986837921140591013)
XLA Ops:
  0.0 8.4 %copy.4 = f32[72,48,384]{0,1,2:T(8,128)} copy(f32[72,48,384]{2,1,0:T(8,128)} %param.2) | data formatting | bytes 10616832 | tf_op args[0]
  8.4 9.6 %copy.5 = f32[4,4,2,72,576]{4,3,2,1,0:T(8,128)} copy(f32[4,4,2,72,576]{3,4,2,1,0:T(8,128)} %bitcast.10) | data formatting | bytes 10616832 | tf_op jit(solution)/shard_map/reshape | solution.py:318
  18.0 3.2 %pad.4.x_ref = f32[4,4,2,72,640]{4,3,2,1,0:T(8,128)S(1)} pad(f32[4,4,2,72,576]{4,3,2,1,0:T(8,128)} %copy.5, f32[]{:T(128)} %constant.2.clone.1), padding=0_0x0_0x0_0x0_0x0_64 | pad | bytes 11206660 | tf_op jit(solution)/shard_map/jit(_pad)/pad | solution.py:319
  21.2 75.1 %shard_map.28 = f32[4,4,2,72,640]{4,3,2,1,0:T(8,128)S(1)} custom-call(f32[4,4,2,72,640]{4,3,2,1,0:T(8,128)S(1)} %pad.4.x_ref), custom_call_target="tpu_custom_call" | custom-call | tf_op jit(solution)/shard_map/pallas_call | solution.py:87
  96.4 1.9 %shard_map.29 = (bf16[1280,640]{1,0:T(8,128)(2,1)S(1)}, bf16[1280,640]{1,0:T(8,128)(2,1)S(1)}) custom-call(f32[2304,640]{1,0:T(8,128)S(1)} %bitcast.9), custom_call_target="tpu_custom_call" | custom-call | tf_op jit(solution)/shard_map/pallas_call | solution.py:143
  98.3 70.7 %shard_map.30 = f32[72,192]{1,0:T(8,128)S(1)} custom-call(bf16[1280,640]{1,0:T(8,128)(2,1)S(1)} %get-tuple-element.7.hi_ref, bf16[1280,640]{1,0:T(8,128)(2,1)S(1)} %get-tuple-element.8.lo_ref, f32[576,1536]{1,0:T(8,128)} %bitcast.11), custom_call_target="tpu_custom_call" | custom-call | tf_op jit(solution)/shard_map/pallas_call | solution.py:290
  168.9 0.6 copy.7

commit v3 on v2

--- a/solution.py
+++ b/solution.py
@@ -28,35 +28,68 @@
     return c[dim], c["y"] * 8 + c["x"] * 2 + c["z"]
 
 
-def exchange_kernel(x_ref, o_ref, g1, g2, ssem, rsem, lsem):
+THIRD = ROWS // 3
+SLAB = 4 * THIRD + 16
+PITCH = 392
+
+
+def exchange_kernel(x_ref, o_ref, x, turned, g0, g1, g2, ssem, rsem, lsem, xsem):
     v = lax.axis_index("vir")
     me = occ_place()
-    third = ROWS // 3
+    reads = [pltpu.make_async_copy(x_ref.at[pl.ds(t * THIRD, THIRD)], x.at[t], xsem.at[t]) for t in range(3)]
+    for c in reads:
+        c.start()
     barrier = pltpu.get_barrier_semaphore()
     for dim in "yxz":
         for k in range(1, SIZE[dim]):
             pl.semaphore_signal(barrier, inc=1, device_id=(occ_peer(me, dim, k)[1], v), device_id_type=MESH)
-    pl.semaphore_wait(barrier, 7)
-
-    def view(ref, t, dim, at, whole):
+
+    lane = lax.broadcasted_iota(jnp.int32, (8, 128), 1)
+
+    def regroup(t, block):
+        @pl.loop(0, 8, unroll=8)
+        def _(p):
+            turned[pl.ds(pl.multiple_of(p * PITCH, 8), 384), 0:O] = x[t, block * 8 + p].T
+
+        @pl.loop(0, 32, unroll=8)
+        def _(to):
+            at = (t, to // 8, lax.rem(to // 2, 4), lax.rem(to, 2))
+            tiles = [jnp.zeros((8, 128), F32)] * 5
+            for d in range(12):
+                tile, off = d * O // 128, d * O % 128
+                piece = turned[pl.ds(to * 12 + d, 8, stride=PITCH), :]
+                if off:
+                    piece = pltpu.roll(piece, off, 1)
+                tiles[tile] = jnp.where((lane >= off) & (lane < off + O), piece, tiles[tile])
+                if off + O > 128:
+                    tiles[tile + 1] = jnp.where(lane < off + O - 128, piece, tiles[tile + 1])
+            for n in range(4):
+                g0[(*at, slice(n * THIRD + block * 8, n * THIRD + block * 8 + 8))] = tiles[n]
+            rest = (*at, slice(4 * THIRD + block // 2 * 8, 4 * THIRD + block // 2 * 8 + 8))
+            if block == 1:
+                g0[rest] = jnp.where(lane < 64, g0[rest], pltpu.roll(tiles[4], 64, 1))
+            else:
+                g0[rest] = tiles[4]
+
+    def view(ref, t, dim, at):
         ix = [slice(None)] * 3
         ix[AXIS[dim]] = at
-        if whole:
-            return ref.at[ix[0], ix[1], ix[2], pl.ds(t * third, third)]
+        if ref is o_ref:
+            return ref.at[ix[0], ix[1], ix[2], t]
         return ref.at[t, ix[0], ix[1], ix[2]]
 
-    held = [(x_ref, True), (g1, False), (g2, False), (o_ref, True)]
+    held = [g0, g1, g2, o_ref]
 
     def start(t, s):
         dim = ORDERS[t][s]
-        (src, src_whole), (dst, dst_whole) = held[s], held[s + 1]
+        src, dst = held[s], held[s + 1]
         copies = []
         for k in range(1, SIZE[dim]):
             at, rank = occ_peer(me, dim, k)
             copies.append(
                 pltpu.make_async_remote_copy(
-                    src_ref=view(src, t, dim, at, src_whole),
-                    dst_ref=view(dst, t, dim, me[dim], dst_whole),
+                    src_ref=view(src, t, dim, at),
+                    dst_ref=view(dst, t, dim, me[dim]),
                     send_sem=ssem.at[t, s, k - 1],
                     recv_sem=rsem.at[t, s, k - 1],
                     device_id=(rank, v),
@@ -64,15 +97,20 @@
                 )
             )
         copies.append(
-            pltpu.make_async_copy(
-                view(src, t, dim, me[dim], src_whole), view(dst, t, dim, me[dim], dst_whole), lsem.at[t, s]
-            )
+            pltpu.make_async_copy(view(src, t, dim, me[dim]), view(dst, t, dim, me[dim]), lsem.at[t, s])
         )
         for c in copies:
             c.start()
         return copies
 
-    flying = [start(t, 0) for t in range(3)]
+    flying = []
+    for t in range(3):
+        reads[t].wait()
+        for block in range(3):
+            regroup(t, block)
+        if t == 0:
+            pl.semaphore_wait(barrier, 7)
+        flying.append(start(t, 0))
     for s in (1, 2, 3):
         following = []
         for t in range(3):
@@ -84,19 +122,24 @@
 
 
 def exchange(x):
+    slabs = pltpu.VMEM((3, 4, 4, 2, SLAB, 128), F32)
     return pl.pallas_call(
         exchange_kernel,
-        out_shape=jax.ShapeDtypeStruct((4, 4, 2, ROWS, WIDE), F32),
+        out_shape=jax.ShapeDtypeStruct((4, 4, 2, 3, SLAB, 128), F32),
         in_specs=[pl.BlockSpec(memory_space=pl.ANY)],
         out_specs=pl.BlockSpec(memory_space=pl.ANY),
         scratch_shapes=[
-            pltpu.VMEM((3, 4, 4, 2, ROWS // 3, WIDE), F32),
-            pltpu.VMEM((3, 4, 4, 2, ROWS // 3, WIDE), F32),
+            pltpu.VMEM((3, THIRD, O, 384), F32),
+            pltpu.VMEM((8 * PITCH, 128), F32),
+            slabs,
+            slabs,
+            slabs,
             pltpu.SemaphoreType.DMA((3, 3, 3)),
             pltpu.SemaphoreType.DMA((3, 3, 3)),
             pltpu.SemaphoreType.DMA((3, 3)),
+            pltpu.SemaphoreType.DMA((3,)),
         ],
-        compiler_params=pltpu.CompilerParams(collective_id=0, has_side_effects=True, vmem_limit_bytes=40 << 20),
+        compiler_params=pltpu.CompilerParams(collective_id=0, has_side_effects=True, vmem_limit_bytes=52 << 20),
     )(x)
 
 
@@ -120,23 +163,43 @@
     return out
 
 
-def pair_sum_kernel(a_any, hi_ref, lo_ref, a_ref, sem):
-    tiles = WIDE // 128
-    copies = [pltpu.make_async_copy(a_any.at[:, pl.ds(t * 128, 128)], a_ref.at[t], sem.at[t]) for t in range(tiles)]
-    for c in copies:
-        c.start()
-    for t in range(tiles):
-        copies[t].wait()
+def pair_sum_kernel(a_any, hi_ref, lo_ref, a_ref, rest, sem):
+    read = pltpu.make_async_copy(a_any, a_ref, sem)
+    read.start()
+    read.wait()
+
+    @pl.loop(0, PAIRS // THIRD, unroll=8)
+    def _(g):
+        both = a_ref[pl.ds(pl.multiple_of(g * SLAB + 4 * THIRD, 8), 8), :]
+        rest[pl.ds(pl.multiple_of(g * THIRD, 8), 8), :] = both
+        rest[pl.ds(pl.multiple_of(g * THIRD + 8, 8), 8), :] = pltpu.roll(both, 64, 1)
+        last = a_ref[pl.ds(pl.multiple_of(g * SLAB + 4 * THIRD + 8, 8), 8), :]
+        rest[pl.ds(pl.multiple_of(g * THIRD + 16, 8), 8), :] = last
+
+    def straight(t, i, j, n):
+        if t == 4:
+            return rest[i * O + j : i * O + j + n, :]
+        at = (2 * i + j // THIRD) * SLAB + t * THIRD + j % THIRD
+        return a_ref[at : at + n, :]
+
+    def mirrored(t, i, j, n):
+        if t == 4:
+            return rest[pl.ds(j * O + i, n, stride=O), :]
+        return a_ref[pl.ds((2 * j + i // THIRD) * SLAB + t * THIRD + i % THIRD, n, stride=2 * SLAB), :]
+
+    for t in range(5):
         for q in range(16):
             rows = []
             for k in range(3):
                 i, m = 3 * q + TURN[k], int(k == 0)
                 rows += [
-                    a_ref[t, i * O + j : i * O + j + n, :] + a_ref[t, pl.ds(j * O + i, n, stride=O), :]
-                    for j, n in runs(3 * q + m, 27 - m)
+                    straight(t, i, j, n) + mirrored(t, i, j, n) for j, n in runs(3 * q + m, 27 - m, THIRD)
                 ]
+            s = jnp.concatenate(rows, axis=0)
+            if t == 4:
+                s = jnp.where(lax.broadcasted_iota(jnp.int32, s.shape, 1) < 64, s, 0)
             at, lanes = slice(q * KEPT, (q + 1) * KEPT), slice(t * 128, (t + 1) * 128)
-            hi_ref[at, lanes], lo_ref[at, lanes] = split(jnp.concatenate(rows, axis=0))
+            hi_ref[at, lanes], lo_ref[at, lanes] = split(s)
 
 
 def pair_sum(a):
@@ -146,8 +209,9 @@
         in_specs=[pl.BlockSpec(memory_space=pl.ANY)],
         out_specs=[pl.BlockSpec(memory_space=pltpu.VMEM)] * 2,
         scratch_shapes=[
-            pltpu.VMEM((WIDE // 128, PAIRS, 128), F32),
-            pltpu.SemaphoreType.DMA((WIDE // 128,)),
+            pltpu.VMEM((32 * 3 * SLAB, 128), F32),
+            pltpu.VMEM((PAIRS, 128), F32),
+            pltpu.SemaphoreType.DMA,
         ],
         compiler_params=pltpu.CompilerParams(vmem_limit_bytes=24 << 20),
     )(a)
@@ -315,9 +379,7 @@
 
 
 def on_device(amplitudes, integrals):
-    slabs = amplitudes.reshape(ROWS, O, 32, 12).transpose(2, 0, 3, 1).reshape(4, 4, 2, ROWS, DEPTH)
-    slabs = jnp.pad(slabs, ((0, 0),) * 4 + ((0, WIDE - DEPTH),))
-    columns = exchange(slabs).reshape(PAIRS, WIDE)
+    columns = exchange(amplitudes).reshape(32 * 3 * SLAB, 128)
     slab_matrix = integrals.transpose(1, 0, 2).reshape(DEPTH, COLS)
     return ladder(*pair_sum(columns), slab_matrix)
 

time: 170 us -> 155 us (0.912)
  local copies, waits for them, and re-layouts: 21.9 us -> 3.19 us
  Pallas kernels: 148 us -> 151 us
    reshape x1 -> x0, local copies, waits for them, and re-layouts: 9.59 us -> none  [on_device(): amplitudes.reshape(ROWS, O, 32, 12).transpose(2, 0, 3, 1)]
    unnamed x2 -> x3, local copies, waits for them, and re-layouts: 9.07 us -> 3.19 us
    pad x1 -> x0, local copies, waits for them, and re-layouts: 3.2 us -> none  [on_device(): slabs = jnp.pad(slabs, ((0, 0),) * 4 + ((0, WIDE - DEPTH),))]
    pallas_call x1, Pallas kernels: 75.1 us -> 77.3 us  [exchange(): pl.pallas_call(exchange_kernel, out_shape=jax.ShapeDtypeStruct((4, 4, 2,...]
where the time goes in v3:
time: 155 us
  Pallas kernels  151 us (97%)
  local copies, waits for them, and re-layouts  3.19 us (2%)
    pallas_call x1, Pallas kernels, exchange(): pl.pallas_call(exchange_kernel, out_shape=jax.ShapeDtypeStruct((4, 4, 2,...  77.3 us
    pallas_call x1, Pallas kernels, ladder(): pl.pallas_call(ladder_kernel, out_shape=jax.ShapeDtypeStruct((ROWS, 192),...  70.6 us
    pallas_call x1, Pallas kernels, pair_sum(): pl.pallas_call(pair_sum_kernel, out_shape=[jax.ShapeDtypeStruct((UNIQUE,...  3.45 us
    unnamed x3, local copies, waits for them, and re-layouts  3.19 us

profile of v3, /device:TPU:32, one launch (start us, length us, event | category | flops | bytes accessed | tf_op | source)
XLA Modules:
  0.0 154.6 jit_solution(17463047569527148603)
XLA Ops:
  0.0 77.3 %shard_map.28 = f32[4,4,2,3,112,128]{5,4,3,2,1,0:T(8,128)} custom-call(f32[72,48,384]{2,1,0:T(8,128)} %x_ref.1), custom_call_target="tpu_custom_call" | custom-call | tf_op jit(solution)/shard_map/pallas_call | solution.py:126
  77.3 0.0 copy-start
  77.3 2.6 %copy-done = f32[4,4,2,3,112,128]{5,4,3,2,1,0:T(8,128)S(1)} copy-done((f32[4,4,2,3,112,128]{5,4,3,2,1,0:T(8,128)S(1)}, f32[4,4,2,3,112,128]{5,4,3,2,1,0:T(8,128)}, u32[]{:S(2)}) %copy-start) | copy-done | bytes 5505048
  79.9 3.5 %shard_map.29 = (bf16[1280,640]{1,0:T(8,128)(2,1)S(1)}, bf16[1280,640]{1,0:T(8,128)(2,1)S(1)}) custom-call(f32[10752,128]{1,0:T(8,128)S(1)} %bitcast.4), custom_call_target="tpu_custom_call" | custom-call | tf_op jit(solution)/shard_map/pallas_call | solution.py:206
  83.3 70.6 %shard_map.30 = f32[72,192]{1,0:T(8,128)S(1)} custom-call(bf16[1280,640]{1,0:T(8,128)(2,1)S(1)} %get-tuple-element.7.hi_ref, bf16[1280,640]{1,0:T(8,128)(2,1)S(1)} %get-tuple-element.8.lo_ref, f32[576,1536]{1,0:T(8,128)} %bitcast.5), custom_call_target="tpu_custom_call" | custom-call | tf_op jit(solution)/shard_map/pallas_call | solution.py:354
  154.0 0.6 copy.4
Async XLA Ops:
  77.3 2.6 %copy-start = (f32[4,4,2,3,112,128]{5,4,3,2,1,0:T(8,128)S(1)}, f32[4,4,2,3,112,128]{5,4,3,2,1,0:T(8,128)}, u32[]{:S(2)}) copy-start(f32[4,4,2,3,112,128]{5,4,3,2,1,0:T(8,128)} %shard_map.28) | copy-start | bytes 16515076

commit v4 on v0

v4 whole, which is shorter than its diff:
```python
import functools

import jax
import jax.numpy as jnp
from jax import lax
from jax.experimental import pallas as pl
from jax.experimental.pallas import tpu as pltpu
from jax.sharding import PartitionSpec as P

O = 48
MESH = pl.DeviceIdType.MESH
F32, BF16 = jnp.float32, jnp.bfloat16
SIZE = {"y": 4, "x": 4, "z": 2}
AXIS = {"y": 0, "x": 1, "z": 2}
ORDERS = (("y", "x", "z"), ("x", "z", "y"), ("z", "y", "x"))
ROWS, DEPTH, WIDE, COLS = 72, 576, 640, 1536
PAIRS = 2304


def occ_place():
    r = lax.axis_index("occ")
    return {"y": r // 8, "x": lax.rem(r // 2, 4), "z": lax.rem(r, 2)}


def occ_peer(me, dim, k):
    c = dict(me)
    c[dim] = lax.rem(me[dim] + k, SIZE[dim])
    return c[dim], c["y"] * 8 + c["x"] * 2 + c["z"]


THIRD = ROWS // 3
BLOCK_AT = (0, 32, 72, 112)
SLAB = BLOCK_AT[3]
PITCH = 392

TURN = (2, 0, 1)
KEPT = 80
UNIQUE = 16 * KEPT


def split(x):
    hi = x.astype(BF16)
    return hi, (x - hi.astype(F32)).astype(BF16)


def ladder_kernel(
    x_ref, b_any, o_ref,
    x, b_ref, turned, g0, g1, g2, g3, rest, s_hi, s_lo, b_hi, b_lo,
    away, other, acc, r1, s1, r2, s2, r3, mine, r4, ends, r5,
    ssem, rsem, lsem, xsem,
):
    v = lax.axis_index("vir")
    r = lax.axis_index("occ")
    core, zh = lax.rem(v, 2), v // 2
    me = occ_place()
    q, zl = r // 2, me["z"]
    reads = [pltpu.make_async_copy(x_ref.at[pl.ds(t * THIRD, THIRD)], x.at[t], xsem.at[t]) for t in range(3)]
    reads.append(pltpu.make_async_copy(b_any, b_ref, xsem.at[3]))
    for c in reads:
        c.start()

    def triple(k):
        return (lax.rem(q + k, 16) * 2 + zl, v)

    def high(k):
        to = lax.rem(zh + k, 4)
        return to, (r, to * 2 + core)

    twin = (r, v + 1 - 2 * core)
    beside = (r + 1 - 2 * zl, v)
    devices = [twin, beside] + [triple(k) for k in range(1, 16)] + [high(k)[1] for k in range(1, 4)]
    barrier = pltpu.get_barrier_semaphore()
    for d in devices:
        pl.semaphore_signal(barrier, inc=1, device_id=d, device_id_type=MESH)

    sent = [0, 0]

    def remote(src, dst, device):
        n = sent[0]
        sent[0] += 1
        c = pltpu.make_async_remote_copy(
            src_ref=src, dst_ref=dst, send_sem=ssem.at[n], recv_sem=rsem.at[n], device_id=device, device_id_type=MESH
        )
        c.start()
        return c

    lane = lax.broadcasted_iota(jnp.int32, (8, 128), 1)

    def regroup(t, block):
        @pl.loop(0, 8, unroll=8)
        def _(p):
            turned[pl.ds(pl.multiple_of(p * PITCH, 8), 384), 0:O] = x[t, block * 8 + p].T

        @pl.loop(0, 32, unroll=8)
        def _(to):
            at = (t, to // 8, lax.rem(to // 2, 4), lax.rem(to, 2))
            tiles = [jnp.zeros((8, 128), F32)] * 5
            for d in range(12):
                tile, off = d * O // 128, d * O % 128
                piece = turned[pl.ds(to * 12 + d, 8, stride=PITCH), :]
                if off:
                    piece = pltpu.roll(piece, off, 1)
                tiles[tile] = jnp.where((lane >= off) & (lane < off + O), piece, tiles[tile])
                if off + O > 128:
                    tiles[tile + 1] = jnp.where(lane < off + O - 128, piece, tiles[tile + 1])
            for n in range(4):
                g0[(*at, slice(BLOCK_AT[block] + 8 * n, BLOCK_AT[block] + 8 * n + 8))] = tiles[n]
            behind = (*at, slice(64, 72) if block < 2 else slice(104, 112))
            if block == 1:
                g0[behind] = jnp.where(lane < 64, g0[behind], pltpu.roll(tiles[4], 64, 1))
            else:
                g0[behind] = tiles[4]

    def view(ref, t, dim, at, rows):
        ix = [slice(None)] * 3
        ix[AXIS[dim]] = at
        if ref is g3:
            return ref.at[ix[0], ix[1], ix[2], t, rows]
        return ref.at[t, ix[0], ix[1], ix[2], rows]

    held = [g0, g1, g2, g3]

    def start(t, s, rows):
        dim = ORDERS[t][s]
        src, dst = held[s], held[s + 1]
        copies = []
        for k in range(1, SIZE[dim]):
            at, rank = occ_peer(me, dim, k)
            copies.append(remote(view(src, t, dim, at, rows), view(dst, t, dim, me[dim], rows), (rank, v)))
        own = pltpu.make_async_copy(
            view(src, t, dim, me[dim], rows), view(dst, t, dim, me[dim], rows), lsem.at[sent[1]]
        )
        sent[1] += 1
        own.start()
        return copies + [own]

    flying = [[], [], []]
    for block in range(3):
        rows = pl.ds(BLOCK_AT[block], BLOCK_AT[block + 1] - BLOCK_AT[block])
        for t in range(3):
            if block == 0:
                reads[t].wait()
            regroup(t, block)
            if block == t == 0:
                pl.semaphore_wait(barrier, len(devices))
            flying[t] += start(t, 0, rows)

    reads[3].wait()

    @pl.loop(0, DEPTH // 48)
    def _(k):
        rows = pl.ds(pl.multiple_of(k * 48, 16), 48)
        b = b_ref[rows, :]
        for c in range(2):
            piece = jnp.concatenate([b[:, e * 384 + c * 192 : e * 384 + c * 192 + 192] for e in range(4)], axis=1)
            for n in range(3):
                b_hi[c * 3 + n, rows, :], b_lo[c * 3 + n, rows, :] = split(piece[:, n * 256 : (n + 1) * 256])

    for s in (1, 2, 3):
        following = []
        for t in range(3):
            for c in flying[t]:
                c.wait()
            if s < 3:
                following.append(start(t, s, pl.ds(0, SLAB)))
        flying = following

    flat = g3.reshape(32 * 3 * SLAB, 128)

    @pl.loop(0, PAIRS // THIRD, unroll=8)
    def _(g):
        both = flat[pl.ds(pl.multiple_of(g * SLAB + 64, 8), 8), :]
        rest[pl.ds(pl.multiple_of(g * THIRD, 8), 8), :] = both
        rest[pl.ds(pl.multiple_of(g * THIRD + 8, 8), 8), :] = pltpu.roll(both, 64, 1)
        rest[pl.ds(pl.multiple_of(g * THIRD + 16, 8), 8), :] = flat[pl.ds(pl.multiple_of(g * SLAB + 104, 8), 8), :]

    def place(t, p):
        return p // THIRD * SLAB + BLOCK_AT[p % THIRD // 8] + t * 8 + p % 8

    def straight(t, i, j, n):
        tiles = []
        for block in range(j // 8, (j + n + 7) // 8):
            p = i * O + block % 6 * 8
            tiles.append(rest[p : p + 8, :] if t == 4 else flat[pl.ds(place(t, p), 8), :])
        return jnp.concatenate(tiles, axis=0)[j % 8 : j % 8 + n]

    def mirrored(t, i, j, n):
        parts = []
        for first, count in ((j, min(n, O - j)), (0, n - min(n, O - j))):
            if count and t == 4:
                parts.append(rest[pl.ds(first * O + i, count, stride=O), :])
            elif count:
                parts.append(flat[pl.ds(place(t, first * O + i), count, stride=2 * SLAB), :])
        return jnp.concatenate(parts, axis=0)

    for t in range(5):
        for own in range(16):
            sums = []
            for k in range(3):
                i, m = 3 * own + TURN[k], int(k == 0)
                sums.append(straight(t, i, 3 * own + m, 27 - m) + mirrored(t, i, 3 * own + m, 27 - m))
            total = jnp.concatenate(sums, axis=0)
            if t == 4:
                total = jnp.where(lax.broadcasted_iota(jnp.int32, total.shape, 1) < 64, total, 0)
            at, lanes = slice(own * KEPT, (own + 1) * KEPT), slice(t * 128, (t + 1) * 128)
            s_hi[at, lanes], s_lo[at, lanes] = split(total)


    def product(n):
        @pl.loop(0, UNIQUE // 256)
        def _(m):
            rows = pl.ds(pl.multiple_of(m * 256, 256), 256)
            dot = functools.partial(jnp.dot, preferred_element_type=F32)

            def multiply(at):
                hi, lo = s_hi[rows, :DEPTH], s_lo[rows, :DEPTH]
                return dot(hi, b_lo[at]) + dot(lo, b_hi[at]) + dot(hi, b_hi[at])

            if n >= 3:
                away[n - 3, rows, :] = multiply((1 - core) * 3 + n - 3)
            else:
                both = multiply(core * 3 + n)
                acc[2 * n, rows, :] = both[:, :128]
                acc[2 * n + 1, rows, :] = both[:, 128:]

    swap, first, second = [], [], []
    for n in (3, 4, 0, 5, 1, 2):
        product(n)
        if n >= 3:
            swap.append(remote(away.at[n - 3], other.at[n - 3], twin))
            continue
        swap[n].wait()

        @pl.loop(0, 16)
        def _(m):
            rows = pl.ds(pl.multiple_of(m * KEPT, 8), KEPT)
            acc[2 * n, rows, :] += other[n, rows, :128]
            acc[2 * n + 1, rows, :] += other[n, rows, 128:]

        copies = []
        for k in range(1, 4):
            at, rank = occ_peer(me, "y", k)
            rows = pl.ds(pl.multiple_of(at * 4 * KEPT, 8), 4 * KEPT)
            copies.append(remote(acc.at[2 * n, rows], r1.at[2 * n, k - 1], (rank, v)))
            at, rank = occ_peer(me, "x", k)
            for y in range(4):
                rows = pl.ds(pl.multiple_of((y * 4 + at) * KEPT, 8), KEPT)
                to = r1.at[2 * n + 1, k - 1, pl.ds(y * KEPT, KEPT)]
                copies.append(remote(acc.at[2 * n + 1, rows], to, (rank, v)))
        first.append(copies)

    for n in range(3):
        for c in first[n]:
            c.wait()
        copies = []
        for h in range(2):
            e = 2 * n + h
            for y in range(4):
                part = pl.ds(y * KEPT, KEPT)
                base = (me["y"] * 4 + y) if h == 0 else (y * 4 + me["x"])
                own = pl.ds(pl.multiple_of(base * KEPT, 8), KEPT)
                s1[e, part, :] = (acc[e, own, :] + r1[e, 0, part, :]) + (r1[e, 1, part, :] + r1[e, 2, part, :])
            for k in range(1, 4):
                at, rank = occ_peer(me, "xy"[h], k)
                rows = pl.ds(pl.multiple_of(at * KEPT, 8), KEPT)
                copies.append(remote(s1.at[e, rows], r2.at[e, k - 1], (rank, v)))
        second.append(copies)

    for n in range(3):
        for c in second[n]:
            c.wait()
        for h in range(2):
            e = 2 * n + h
            own = pl.ds(pl.multiple_of(me["xy"[h]] * KEPT, 8), KEPT)
            s2[e] = (s1[e, own, :] + r2[e, 0]) + (r2[e, 1] + r2[e, 2])

    def part(to):
        return s2.at[pl.ds(to // 2 * 3 + lax.rem(to, 2), 2)]

    third = [remote(part(high(k)[0]), r3.at[k - 1], high(k)[1]) for k in range(1, 4)]
    total = part(zh)[...]
    for k in range(1, 4):
        third[k - 1].wait()
        total += r3[k - 1]
    total = jnp.concatenate([total[0], total[1]], axis=1)
    mine[...] = jnp.where(lax.rem(zh, 2) == 0, total[:, :192], total[:, 64:])
    fourth = remote(mine, r4, beside)
    fourth.wait()
    u = mine[...] + r4[...]

    def kept(k, m):
        return u[27 * k - 1 + m : 27 * k + m]

    fifth = []
    for k in range(1, 8):
        ends[k - 1, :9] = jnp.concatenate([kept(e, 3 * k + t) for t in range(3) for e in (1, 2, 0)], axis=0)
        fifth.append(remote(ends.at[k - 1], r5.at[k - 1], triple(k)))
    for c in fifth:
        c.wait()
    turned = []
    for t in range(3):
        k = TURN.index(t)
        rows = [u[27 * k - 1 : 27 * k + 26]] if k else [kept(1, 2), u[0:26]]
        rows += [r5[6 - e, 3 * t : 3 * t + 3] for e in range(7)]
        turned.append(pltpu.roll(jnp.concatenate(rows, axis=0), 3 * q, 0))
    low = jnp.concatenate([turned[0], turned[1][:24]], axis=0)
    top = jnp.concatenate([turned[1][24:], turned[2]], axis=0)
    o_ref[...] = jnp.where(zl == 0, low, top)


def ladder(x, b):
    slabs = pltpu.VMEM((3, 4, 4, 2, SLAB, 128), F32)
    return pl.pallas_call(
        ladder_kernel,
        out_shape=jax.ShapeDtypeStruct((ROWS, 192), F32),
        in_specs=[pl.BlockSpec(memory_space=pl.ANY)] * 2,
        out_specs=pl.BlockSpec(memory_space=pltpu.VMEM),
        scratch_shapes=[
            pltpu.VMEM((3, THIRD, O, 384), F32),
            pltpu.VMEM((DEPTH, COLS), F32),
            pltpu.VMEM((8 * PITCH, 128), F32),
            slabs,
            slabs,
            slabs,
            pltpu.VMEM((4, 4, 2, 3, SLAB, 128), F32),
            pltpu.VMEM((PAIRS, 128), F32),
            pltpu.VMEM((UNIQUE, WIDE), BF16),
            pltpu.VMEM((UNIQUE, WIDE), BF16),
            pltpu.VMEM((6, DEPTH, 256), BF16),
            pltpu.VMEM((6, DEPTH, 256), BF16),
            pltpu.VMEM((3, UNIQUE, 256), F32),
            pltpu.VMEM((3, UNIQUE, 256), F32),
            pltpu.VMEM((6, UNIQUE, 128), F32),
            pltpu.VMEM((6, 3, 4 * KEPT, 128), F32),
            pltpu.VMEM((6, 4 * KEPT, 128), F32),
            pltpu.VMEM((6, 3, KEPT, 128), F32),
            pltpu.VMEM((6, KEPT, 128), F32),
            pltpu.VMEM((3, 2, KEPT, 128), F32),
            pltpu.VMEM((KEPT, 192), F32),
            pltpu.VMEM((KEPT, 192), F32),
            pltpu.VMEM((7, 16, 192), F32),
            pltpu.VMEM((7, 16, 192), F32),
            pltpu.SemaphoreType.DMA((112,)),
            pltpu.SemaphoreType.DMA((112,)),
            pltpu.SemaphoreType.DMA((15,)),
            pltpu.SemaphoreType.DMA((4,)),
        ],
        compiler_params=pltpu.CompilerParams(collective_id=0, has_side_effects=True, vmem_limit_bytes=62 << 20),
    )(x, b)


def on_device(amplitudes, integrals):
    slab_matrix = integrals.transpose(1, 0, 2).reshape(DEPTH, COLS)
    return ladder(amplitudes, slab_matrix)


def solution(mesh):
    in_specs = (P("occ", "vir", None), P("vir", "occ", None))
    out_specs = P("occ", "vir")
    return jax.shard_map(
        on_device, mesh=mesh, in_specs=in_specs, out_specs=out_specs, check_vma=False
    )
```

time: 645 us -> 138 us (0.21)
  waiting for transfers between devices: 491 us -> 0 us
  Pallas kernels: 0 us -> 136 us
  local copies, waits for them, and re-layouts: 76.2 us -> 1.52 us
  matrix products: 37.5 us -> 0 us
  other arithmetic: 15.2 us -> 0 us
  between operations: 13.4 us -> 0.01 us
  starting transfers between devices: 8.94 us -> 0 us
    reduce_scatter x1 -> x0, waiting for transfers between devices: 316 us -> none  [on_device(): lax.psum_scatter(jnp.dot(summed, slab_matrix, precision=lax.Precision.HIG...]
    all_to_all x1 -> x0, waiting for transfers between devices: 136 us -> none  [on_device(): lax.all_to_all(amplitudes, 'occ', split_axis=2, concat_axis=0, tiled=True)]
    pallas_call x0 -> x1, Pallas kernels: none -> 136 us  [ladder(): pl.pallas_call(ladder_kernel, out_shape=jax.ShapeDtypeStruct((ROWS, 192),...]
    unnamed x3 -> x0, waiting for transfers between devices: 38.9 us -> none
    dot_general x1 -> x0, matrix products: 37.5 us -> none  [on_device(): jnp.dot(summed, slab_matrix, precision=lax.Precision.HIGHEST, preferred_e...]
    another operation x2 -> x0, local copies, waits for them, and re-layouts: 30 us -> none  [on_device(): grouped = flattened.reshape(O, O, col_count)]
    add x1 -> x0, other arithmetic: 15.2 us -> none  [on_device(): grouped + jnp.transpose(grouped, (1, 0, 2))]
    unnamed x6 -> x1, local copies, waits for them, and re-layouts: 16.4 us -> 1.52 us
  transfers between devices with their start and end apart: 3 -> 0, of which waited for: 3 -> 0; matrix products, arithmetic and copies ran while one was open for 1% -> 0% of each run, Pallas kernels for 0% -> 0%
where the time goes in v4:
time: 138 us
  Pallas kernels  136 us (99%)
  local copies, waits for them, and re-layouts  1.52 us (1%)
    pallas_call x1, Pallas kernels, ladder(): pl.pallas_call(ladder_kernel, out_shape=jax.ShapeDtypeStruct((ROWS, 192),...  136 us

profile of v4, /device:TPU:32, one launch (start us, length us, event | category | flops | bytes accessed | tf_op | source)
XLA Modules:
  0.0 137.7 jit_solution(616104041171159585)
XLA Ops:
  0.0 136.2 %shard_map.28 = f32[72,192]{1,0:T(8,128)} custom-call(f32[72,48,384]{2,1,0:T(8,128)} %x_ref.1, f32[576,1536]{1,0:T(8,128)} %bitcast.3), custom_call_target="tpu_custom_call" | custom-call | tf_op jit(solution)/shard_map/pallas_call | solution.py:313
  136.2 1.5 %copy.4 = f32[72,192]{1,0:T(8,128)} copy(f32[72,192]{1,0:T(8,128)} %shard_map.28) | data formatting | bytes 110592

commit v5 on v4

--- a/solution.py
+++ b/solution.py
@@ -36,6 +36,7 @@
 TURN = (2, 0, 1)
 KEPT = 80
 UNIQUE = 16 * KEPT
+CHUNK = 640
 
 
 def split(x):
@@ -47,7 +48,7 @@
     x_ref, b_any, o_ref,
     x, b_ref, turned, g0, g1, g2, g3, rest, s_hi, s_lo, b_hi, b_lo,
     away, other, acc, r1, s1, r2, s2, r3, mine, r4, ends, r5,
-    ssem, rsem, lsem, xsem,
+    ssem, rsem, lsem, xsem, zsem,
 ):
     v = lax.axis_index("vir")
     r = lax.axis_index("occ")
@@ -62,13 +63,9 @@
     def triple(k):
         return (lax.rem(q + k, 16) * 2 + zl, v)
 
-    def high(k):
-        to = lax.rem(zh + k, 4)
-        return to, (r, to * 2 + core)
-
     twin = (r, v + 1 - 2 * core)
     beside = (r + 1 - 2 * zl, v)
-    devices = [twin, beside] + [triple(k) for k in range(1, 16)] + [high(k)[1] for k in range(1, 4)]
+    devices = [twin, beside] + [triple(k) for k in range(1, 16)] + [(r, lax.rem(zh + k, 4) * 2 + core) for k in range(1, 4)]
     barrier = pltpu.get_barrier_semaphore()
     for d in devices:
         pl.semaphore_signal(barrier, inc=1, device_id=d, device_id_type=MESH)
@@ -120,8 +117,9 @@
 
     held = [g0, g1, g2, g3]
 
-    def start(t, s, rows):
+    def start(t, s, block):
         dim = ORDERS[t][s]
+        rows = pl.ds(BLOCK_AT[block], BLOCK_AT[block + 1] - BLOCK_AT[block])
         src, dst = held[s], held[s + 1]
         copies = []
         for k in range(1, SIZE[dim]):
@@ -134,16 +132,25 @@
         own.start()
         return copies + [own]
 
-    flying = [[], [], []]
+    flying = {}
     for block in range(3):
-        rows = pl.ds(BLOCK_AT[block], BLOCK_AT[block + 1] - BLOCK_AT[block])
         for t in range(3):
             if block == 0:
                 reads[t].wait()
             regroup(t, block)
             if block == t == 0:
                 pl.semaphore_wait(barrier, len(devices))
-            flying[t] += start(t, 0, rows)
+            flying[t, block] = start(t, 0, block)
+
+    def onward(s):
+        for block in range(3):
+            for t in range(3):
+                for c in flying[t, block]:
+                    c.wait()
+                if s < 3:
+                    flying[t, block] = start(t, s, block)
+
+    onward(1)
 
     reads[3].wait()
 
@@ -156,14 +163,8 @@
             for n in range(3):
                 b_hi[c * 3 + n, rows, :], b_lo[c * 3 + n, rows, :] = split(piece[:, n * 256 : (n + 1) * 256])
 
-    for s in (1, 2, 3):
-        following = []
-        for t in range(3):
-            for c in flying[t]:
-                c.wait()
-            if s < 3:
-                following.append(start(t, s, pl.ds(0, SLAB)))
-        flying = following
+    onward(2)
+    onward(3)
 
     flat = g3.reshape(32 * 3 * SLAB, 128)
 
@@ -207,9 +208,9 @@
 
 
     def product(n):
-        @pl.loop(0, UNIQUE // 256)
+        @pl.loop(0, UNIQUE // CHUNK)
         def _(m):
-            rows = pl.ds(pl.multiple_of(m * 256, 256), 256)
+            rows = pl.ds(pl.multiple_of(m * CHUNK, 128), CHUNK)
             dot = functools.partial(jnp.dot, preferred_element_type=F32)
 
             def multiply(at):
@@ -266,6 +267,7 @@
                 copies.append(remote(s1.at[e, rows], r2.at[e, k - 1], (rank, v)))
         second.append(copies)
 
+    third = []
     for n in range(3):
         for c in second[n]:
             c.wait()
@@ -273,15 +275,32 @@
             e = 2 * n + h
             own = pl.ds(pl.multiple_of(me["xy"[h]] * KEPT, 8), KEPT)
             s2[e] = (s1[e, own, :] + r2[e, 0]) + (r2[e, 1] + r2[e, 2])
-
-    def part(to):
-        return s2.at[pl.ds(to // 2 * 3 + lax.rem(to, 2), 2)]
-
-    third = [remote(part(high(k)[0]), r3.at[k - 1], high(k)[1]) for k in range(1, 4)]
-    total = part(zh)[...]
-    for k in range(1, 4):
-        third[k - 1].wait()
-        total += r3[k - 1]
+            for half in range(2):
+                if e % 3 == 2 - 2 * half:
+                    continue
+                to = e // 3 * 2 + half
+                slot, k = e % 3 - half, lax.rem(zh - to + 4, 4)
+                c = pltpu.make_async_remote_copy(
+                    src_ref=s2.at[e],
+                    dst_ref=r3.at[slot, lax.max(k - 1, 0)],
+                    send_sem=ssem.at[sent[0]],
+                    recv_sem=zsem.at[slot, lax.max(k - 1, 0)],
+                    device_id=(r, to * 2 + core),
+                    device_id_type=MESH,
+                )
+                sent[0] += 1
+                third.append((to, c))
+                pl.when(zh != to)(c.start)
+    for to, c in third:
+        pl.when(zh != to)(c.wait_send)
+    total = s2[pl.ds(zh // 2 * 3 + lax.rem(zh, 2), 2)]
+    for k in range(3):
+        for slot in range(2):
+            pltpu.make_async_remote_copy(
+                src_ref=s2.at[slot], dst_ref=r3.at[slot, k], send_sem=ssem.at[0], recv_sem=zsem.at[slot, k],
+                device_id=twin, device_id_type=MESH,
+            ).wait_recv()
+        total += r3[:, k]
     total = jnp.concatenate([total[0], total[1]], axis=1)
     mine[...] = jnp.where(lax.rem(zh, 2) == 0, total[:, :192], total[:, 64:])
     fourth = remote(mine, r4, beside)
@@ -335,15 +354,16 @@
             pltpu.VMEM((6, 4 * KEPT, 128), F32),
             pltpu.VMEM((6, 3, KEPT, 128), F32),
             pltpu.VMEM((6, KEPT, 128), F32),
-            pltpu.VMEM((3, 2, KEPT, 128), F32),
+            pltpu.VMEM((2, 3, KEPT, 128), F32),
             pltpu.VMEM((KEPT, 192), F32),
             pltpu.VMEM((KEPT, 192), F32),
             pltpu.VMEM((7, 16, 192), F32),
             pltpu.VMEM((7, 16, 192), F32),
-            pltpu.SemaphoreType.DMA((112,)),
-            pltpu.SemaphoreType.DMA((112,)),
-            pltpu.SemaphoreType.DMA((15,)),
+            pltpu.SemaphoreType.DMA((145,)),
+            pltpu.SemaphoreType.DMA((145,)),
+            pltpu.SemaphoreType.DMA((27,)),
             pltpu.SemaphoreType.DMA((4,)),
+            pltpu.SemaphoreType.DMA((2, 3)),
         ],
         compiler_params=pltpu.CompilerParams(collective_id=0, has_side_effects=True, vmem_limit_bytes=62 << 20),
     )(x, b)

time: 138 us -> 129 us (0.935)
  Pallas kernels: 136 us -> 127 us
    pallas_call x1, Pallas kernels: 136 us -> 127 us  [ladder(): pl.pallas_call(ladder_kernel, out_shape=jax.ShapeDtypeStruct((ROWS, 192),...]
where the time goes in v5:
time: 129 us
  Pallas kernels  127 us (98%)
  local copies, waits for them, and re-layouts  1.52 us (1%)
    pallas_call x1, Pallas kernels, ladder(): pl.pallas_call(ladder_kernel, out_shape=jax.ShapeDtypeStruct((ROWS, 192),...  127 us

profile of v5, /device:TPU:32, one launch (start us, length us, event | category | flops | bytes accessed | tf_op | source)
XLA Modules:
  0.0 129.0 jit_solution(6751681523480825346)
XLA Ops:
  0.0 127.5 %shard_map.28 = f32[72,192]{1,0:T(8,128)} custom-call(f32[72,48,384]{2,1,0:T(8,128)} %x_ref.1, f32[576,1536]{1,0:T(8,128)} %bitcast.3), custom_call_target="tpu_custom_call" | custom-call | tf_op jit(solution)/shard_map/pallas_call | solution.py:332
  127.5 1.5 %copy.4 = f32[72,192]{1,0:T(8,128)} copy(f32[72,192]{1,0:T(8,128)} %shard_map.28) | data formatting | bytes 110592

commit v6 on v5

--- a/solution.py
+++ b/solution.py
@@ -224,8 +224,45 @@
                 acc[2 * n, rows, :] = both[:, :128]
                 acc[2 * n + 1, rows, :] = both[:, 128:]
 
+    def ring(src, landing, dim, pieces):
+        up, up_rank = occ_peer(me, dim, 1)
+        down, down_rank = occ_peer(me, dim, 3)
+        far, _ = occ_peer(me, dim, 2)
+
+        def send(at, half, rank, slot):
+            return [
+                remote(src.at[pl.ds(begin, n)], landing.at[slot, pl.ds(to, n)], (rank, v))
+                for begin, to, n in pieces(at, half)
+            ]
+
+        relays = send(far, 0, up_rank, 2) + send(far, 1, down_rank, 2)
+        direct = send(up, 1, up_rank, 0) + send(down, 0, down_rank, 1)
+
+        def forward():
+            for c in relays:
+                c.wait()
+            for at, half in ((up, 0), (down, 1)):
+                for begin, to, n in pieces(at, half):
+                    src[pl.ds(begin, n), :] += landing[2, pl.ds(to, n), :]
+            direct.extend(send(up, 0, up_rank, 0) + send(down, 1, down_rank, 1))
+
+        def finish():
+            for c in direct:
+                c.wait()
+
+        return forward, finish
+
+    def of_y(at, half):
+        return [(pl.multiple_of((at * 4 + 2 * half) * KEPT, 8), 2 * half * KEPT, 2 * KEPT)]
+
+    def of_x(at, half):
+        return [(pl.multiple_of((y * 4 + at) * KEPT, 8), y * KEPT, KEPT) for y in (2 * half, 2 * half + 1)]
+
+    def of_rest(at, half):
+        return [(pl.multiple_of(at * KEPT + half * (KEPT // 2), 8), half * (KEPT // 2), KEPT // 2)]
+
     swap, first, second = [], [], []
-    for n in (3, 4, 0, 5, 1, 2):
+    for n in (3, 0, 4, 1, 5, 2):
         product(n)
         if n >= 3:
             swap.append(remote(away.at[n - 3], other.at[n - 3], twin))
@@ -238,43 +275,35 @@
             acc[2 * n, rows, :] += other[n, rows, :128]
             acc[2 * n + 1, rows, :] += other[n, rows, 128:]
 
-        copies = []
-        for k in range(1, 4):
-            at, rank = occ_peer(me, "y", k)
-            rows = pl.ds(pl.multiple_of(at * 4 * KEPT, 8), 4 * KEPT)
-            copies.append(remote(acc.at[2 * n, rows], r1.at[2 * n, k - 1], (rank, v)))
-            at, rank = occ_peer(me, "x", k)
+        first += [ring(acc.at[e], r1.at[e], "yx"[e % 2], (of_y, of_x)[e % 2]) for e in (2 * n, 2 * n + 1)]
+        if n:
+            first[2 * n - 2][0]()
+            first[2 * n - 1][0]()
+    first[4][0]()
+    first[5][0]()
+
+    for n in range(3):
+        for e in (2 * n, 2 * n + 1):
+            first[e][1]()
             for y in range(4):
-                rows = pl.ds(pl.multiple_of((y * 4 + at) * KEPT, 8), KEPT)
-                to = r1.at[2 * n + 1, k - 1, pl.ds(y * KEPT, KEPT)]
-                copies.append(remote(acc.at[2 * n + 1, rows], to, (rank, v)))
-        first.append(copies)
-
+                part = pl.ds(y * KEPT, KEPT)
+                base = (me["y"] * 4 + y) if e % 2 == 0 else (y * 4 + me["x"])
+                own = pl.ds(pl.multiple_of(base * KEPT, 8), KEPT)
+                s1[e, part, :] = acc[e, own, :] + (r1[e, 0, part, :] + r1[e, 1, part, :])
+            second.append(ring(s1.at[e], r2.at[e], "xy"[e % 2], of_rest))
+        if n:
+            second[2 * n - 2][0]()
+            second[2 * n - 1][0]()
+    second[4][0]()
+    second[5][0]()
+
+    third = []
     for n in range(3):
-        for c in first[n]:
-            c.wait()
-        copies = []
         for h in range(2):
             e = 2 * n + h
-            for y in range(4):
-                part = pl.ds(y * KEPT, KEPT)
-                base = (me["y"] * 4 + y) if h == 0 else (y * 4 + me["x"])
-                own = pl.ds(pl.multiple_of(base * KEPT, 8), KEPT)
-                s1[e, part, :] = (acc[e, own, :] + r1[e, 0, part, :]) + (r1[e, 1, part, :] + r1[e, 2, part, :])
-            for k in range(1, 4):
-                at, rank = occ_peer(me, "xy"[h], k)
-                rows = pl.ds(pl.multiple_of(at * KEPT, 8), KEPT)
-                copies.append(remote(s1.at[e, rows], r2.at[e, k - 1], (rank, v)))
-        second.append(copies)
-
-    third = []
-    for n in range(3):
-        for c in second[n]:
-            c.wait()
-        for h in range(2):
-            e = 2 * n + h
+            second[e][1]()
             own = pl.ds(pl.multiple_of(me["xy"[h]] * KEPT, 8), KEPT)
-            s2[e] = (s1[e, own, :] + r2[e, 0]) + (r2[e, 1] + r2[e, 2])
+            s2[e] = s1[e, own, :] + (r2[e, 0] + r2[e, 1])
             for half in range(2):
                 if e % 3 == 2 - 2 * half:
                     continue
@@ -359,8 +388,8 @@
             pltpu.VMEM((KEPT, 192), F32),
             pltpu.VMEM((7, 16, 192), F32),
             pltpu.VMEM((7, 16, 192), F32),
-            pltpu.SemaphoreType.DMA((145,)),
-            pltpu.SemaphoreType.DMA((145,)),
+            pltpu.SemaphoreType.DMA((172,)),
+            pltpu.SemaphoreType.DMA((172,)),
             pltpu.SemaphoreType.DMA((27,)),
             pltpu.SemaphoreType.DMA((4,)),
             pltpu.SemaphoreType.DMA((2, 3)),

time: 129 us -> 127 us (0.984)
  Pallas kernels: 127 us -> 125 us
    pallas_call x1, Pallas kernels: 127 us -> 125 us  [ladder(): pl.pallas_call(ladder_kernel, out_shape=jax.ShapeDtypeStruct((ROWS, 192),...]
where the time goes in v6:
time: 127 us; the launch traced here: 126 us
  Pallas kernels  125 us (98%)
  local copies, waits for them, and re-layouts  1.52 us (1%)
    pallas_call x1, Pallas kernels, ladder(): pl.pallas_call(ladder_kernel, out_shape=jax.ShapeDtypeStruct((ROWS, 192),...  125 us

profile of v6, /device:TPU:32, one launch (start us, length us, event | category | flops | bytes accessed | tf_op | source)
XLA Modules:
  0.0 126.3 jit_solution(2411692888930356811)
XLA Ops:
  0.0 124.7 %shard_map.28 = f32[72,192]{1,0:T(8,128)} custom-call(f32[72,48,384]{2,1,0:T(8,128)} %x_ref.1, f32[576,1536]{1,0:T(8,128)} %bitcast.3), custom_call_target="tpu_custom_call" | custom-call | tf_op jit(solution)/shard_map/pallas_call | solution.py:361
  124.7 1.5 %copy.4 = f32[72,192]{1,0:T(8,128)} copy(f32[72,192]{1,0:T(8,128)} %shard_map.28) | data formatting | bytes 110592

commit v7 on v6

--- a/solution.py
+++ b/solution.py
@@ -1,5 +1,3 @@
-import functools
-
 import jax
 import jax.numpy as jnp
 from jax import lax
@@ -13,7 +11,7 @@
 SIZE = {"y": 4, "x": 4, "z": 2}
 AXIS = {"y": 0, "x": 1, "z": 2}
 ORDERS = (("y", "x", "z"), ("x", "z", "y"), ("z", "y", "x"))
-ROWS, DEPTH, WIDE, COLS = 72, 576, 640, 1536
+ROWS, DEPTH, COLS = 72, 576, 1536
 PAIRS = 2304
 
 
@@ -46,7 +44,7 @@
 
 def ladder_kernel(
     x_ref, b_any, o_ref,
-    x, b_ref, turned, g0, g1, g2, g3, rest, s_hi, s_lo, b_hi, b_lo,
+    x, b_ref, turned, g0, g1, g2, g3, rest, s_hi, s_lo, s_mix, b_hi, b_lo,
     away, other, acc, r1, s1, r2, s2, r3, mine, r4, ends, r5,
     ssem, rsem, lsem, xsem, zsem,
 ):
@@ -55,10 +53,15 @@
     core, zh = lax.rem(v, 2), v // 2
     me = occ_place()
     q, zl = r // 2, me["z"]
-    reads = [pltpu.make_async_copy(x_ref.at[pl.ds(t * THIRD, THIRD)], x.at[t], xsem.at[t]) for t in range(3)]
-    reads.append(pltpu.make_async_copy(b_any, b_ref, xsem.at[3]))
-    for c in reads:
-        c.start()
+    reads = {}
+    for block in range(3):
+        for t in range(3):
+            rows = pl.ds(t * THIRD + block * 8, 8)
+            reads[t, block] = pltpu.make_async_copy(
+                x_ref.at[rows], x.at[t, pl.ds(block * 8, 8)], xsem.at[block * 3 + t]
+            )
+            reads[t, block].start()
+    read_b = pltpu.make_async_copy(b_any, b_ref, xsem.at[9])
 
     def triple(k):
         return (lax.rem(q + k, 16) * 2 + zl, v)
@@ -135,10 +138,10 @@
     flying = {}
     for block in range(3):
         for t in range(3):
-            if block == 0:
-                reads[t].wait()
+            reads[t, block].wait()
             regroup(t, block)
             if block == t == 0:
+                read_b.start()
                 pl.semaphore_wait(barrier, len(devices))
             flying[t, block] = start(t, 0, block)
 
@@ -152,7 +155,7 @@
 
     onward(1)
 
-    reads[3].wait()
+    read_b.wait()
 
     @pl.loop(0, DEPTH // 48)
     def _(k):
@@ -201,21 +204,31 @@
                 i, m = 3 * own + TURN[k], int(k == 0)
                 sums.append(straight(t, i, 3 * own + m, 27 - m) + mirrored(t, i, 3 * own + m, 27 - m))
             total = jnp.concatenate(sums, axis=0)
-            if t == 4:
-                total = jnp.where(lax.broadcasted_iota(jnp.int32, total.shape, 1) < 64, total, 0)
             at, lanes = slice(own * KEPT, (own + 1) * KEPT), slice(t * 128, (t + 1) * 128)
-            s_hi[at, lanes], s_lo[at, lanes] = split(total)
+            if t < 4:
+                s_hi[at, lanes], s_lo[at, lanes] = split(total)
+            else:
+                high = total.astype(BF16).astype(F32)
+                low = pltpu.roll(total - high, 64, 1)
+                left = lax.broadcasted_iota(jnp.int32, total.shape, 1) < 64
+                s_mix[at, :] = jnp.where(left, high, low).astype(BF16)
 
 
     def product(n):
         @pl.loop(0, UNIQUE // CHUNK)
         def _(m):
             rows = pl.ds(pl.multiple_of(m * CHUNK, 128), CHUNK)
-            dot = functools.partial(jnp.dot, preferred_element_type=F32)
 
             def multiply(at):
-                hi, lo = s_hi[rows, :DEPTH], s_lo[rows, :DEPTH]
-                return dot(hi, b_lo[at]) + dot(lo, b_hi[at]) + dot(hi, b_hi[at])
+                hi, lo, mix = s_hi[rows, :], s_lo[rows, :], s_mix[rows, :]
+                hi_top, hi_end = b_hi[at, :512], b_hi[at, 512:]
+                lo_top, lo_end = b_lo[at, :512], b_lo[at, 512:]
+                none = jnp.zeros_like(lo_end)
+                return jnp.dot(
+                    jnp.concatenate([hi, mix, lo, hi, mix], axis=1),
+                    jnp.concatenate([hi_top, hi_end, hi_end, hi_top, lo_top, lo_end, none], axis=0),
+                    preferred_element_type=F32,
+                )
 
             if n >= 3:
                 away[n - 3, rows, :] = multiply((1 - core) * 3 + n - 3)
@@ -257,9 +270,6 @@
 
     def of_x(at, half):
         return [(pl.multiple_of((y * 4 + at) * KEPT, 8), y * KEPT, KEPT) for y in (2 * half, 2 * half + 1)]
-
-    def of_rest(at, half):
-        return [(pl.multiple_of(at * KEPT + half * (KEPT // 2), 8), half * (KEPT // 2), KEPT // 2)]
 
     swap, first, second = [], [], []
     for n in (3, 0, 4, 1, 5, 2):
@@ -290,20 +300,21 @@
                 base = (me["y"] * 4 + y) if e % 2 == 0 else (y * 4 + me["x"])
                 own = pl.ds(pl.multiple_of(base * KEPT, 8), KEPT)
                 s1[e, part, :] = acc[e, own, :] + (r1[e, 0, part, :] + r1[e, 1, part, :])
-            second.append(ring(s1.at[e], r2.at[e], "xy"[e % 2], of_rest))
-        if n:
-            second[2 * n - 2][0]()
-            second[2 * n - 1][0]()
-    second[4][0]()
-    second[5][0]()
+            copies = []
+            for k in range(1, 4):
+                at, rank = occ_peer(me, "xy"[e % 2], k)
+                rows = pl.ds(pl.multiple_of(at * KEPT, 8), KEPT)
+                copies.append(remote(s1.at[e, rows], r2.at[e, k - 1], (rank, v)))
+            second.append(copies)
 
     third = []
     for n in range(3):
         for h in range(2):
             e = 2 * n + h
-            second[e][1]()
+            for c in second[e]:
+                c.wait()
             own = pl.ds(pl.multiple_of(me["xy"[h]] * KEPT, 8), KEPT)
-            s2[e] = s1[e, own, :] + (r2[e, 0] + r2[e, 1])
+            s2[e] = (s1[e, own, :] + r2[e, 0]) + (r2[e, 1] + r2[e, 2])
             for half in range(2):
                 if e % 3 == 2 - 2 * half:
                     continue
@@ -372,8 +383,9 @@
             slabs,
             pltpu.VMEM((4, 4, 2, 3, SLAB, 128), F32),
             pltpu.VMEM((PAIRS, 128), F32),
-            pltpu.VMEM((UNIQUE, WIDE), BF16),
-            pltpu.VMEM((UNIQUE, WIDE), BF16),
+            pltpu.VMEM((UNIQUE, 512), BF16),
+            pltpu.VMEM((UNIQUE, 512), BF16),
+            pltpu.VMEM((UNIQUE, 128), BF16),
             pltpu.VMEM((6, DEPTH, 256), BF16),
             pltpu.VMEM((6, DEPTH, 256), BF16),
             pltpu.VMEM((3, UNIQUE, 256), F32),
@@ -388,10 +400,10 @@
             pltpu.VMEM((KEPT, 192), F32),
             pltpu.VMEM((7, 16, 192), F32),
             pltpu.VMEM((7, 16, 192), F32),
-            pltpu.SemaphoreType.DMA((172,)),
-            pltpu.SemaphoreType.DMA((172,)),
+            pltpu.SemaphoreType.DMA((154,)),
+            pltpu.SemaphoreType.DMA((154,)),
             pltpu.SemaphoreType.DMA((27,)),
-            pltpu.SemaphoreType.DMA((4,)),
+            pltpu.SemaphoreType.DMA((10,)),
             pltpu.SemaphoreType.DMA((2, 3)),
         ],
         compiler_params=pltpu.CompilerParams(collective_id=0, has_side_effects=True, vmem_limit_bytes=62 << 20),

time: 127 us -> 126 us (level)
  no operation moved by 1% of the time
where the time goes in v7:
time: 126 us
  Pallas kernels  124 us (98%)
  local copies, waits for them, and re-layouts  1.52 us (1%)
    pallas_call x1, Pallas kernels, ladder(): pl.pallas_call(ladder_kernel, out_shape=jax.ShapeDtypeStruct((ROWS, 192),...  124 us

profile of v7, /device:TPU:32, one launch (start us, length us, event | category | flops | bytes accessed | tf_op | source)
XLA Modules:
  0.0 125.6 jit_solution(7336077145464486355)
XLA Ops:
  0.0 124.1 %shard_map.28 = f32[72,192]{1,0:T(8,128)} custom-call(f32[72,48,384]{2,1,0:T(8,128)} %x_ref.1, f32[576,1536]{1,0:T(8,128)} %bitcast.3), custom_call_target="tpu_custom_call" | custom-call | tf_op jit(solution)/shard_map/pallas_call | solution.py:372
  124.1 1.5 %copy.4 = f32[72,192]{1,0:T(8,128)} copy(f32[72,192]{1,0:T(8,128)} %shard_map.28) | data formatting | bytes 110592

commit v8 on v7

--- a/solution.py
+++ b/solution.py
@@ -272,7 +272,7 @@
         return [(pl.multiple_of((y * 4 + at) * KEPT, 8), y * KEPT, KEPT) for y in (2 * half, 2 * half + 1)]
 
     swap, first, second = [], [], []
-    for n in (3, 0, 4, 1, 5, 2):
+    for n in (3, 4, 0, 5, 1, 2):
         product(n)
         if n >= 3:
             swap.append(remote(away.at[n - 3], other.at[n - 3], twin))

time: 126 us -> 125 us (level)
  no operation moved by 1% of the time
where the time goes in v8:
time: 125 us; the launch traced here: 124 us
  Pallas kernels  123 us (98%)
  local copies, waits for them, and re-layouts  1.52 us (1%)
    pallas_call x1, Pallas kernels, ladder(): pl.pallas_call(ladder_kernel, out_shape=jax.ShapeDtypeStruct((ROWS, 192),...  123 us

profile of v8, /device:TPU:32, one launch (start us, length us, event | category | flops | bytes accessed | tf_op | source)
XLA Modules:
  0.0 124.4 jit_solution(5788294305692008475)
XLA Ops:
  0.0 122.9 %shard_map.28 = f32[72,192]{1,0:T(8,128)} custom-call(f32[72,48,384]{2,1,0:T(8,128)} %x_ref.1, f32[576,1536]{1,0:T(8,128)} %bitcast.3), custom_call_target="tpu_custom_call" | custom-call | tf_op jit(solution)/shard_map/pallas_call | solution.py:372
  122.9 1.5 %copy.4 = f32[72,192]{1,0:T(8,128)} copy(f32[72,192]{1,0:T(8,128)} %shard_map.28) | data formatting | bytes 110592

commit v9 on v8

--- a/solution.py
+++ b/solution.py
@@ -157,7 +157,7 @@
 
     read_b.wait()
 
-    @pl.loop(0, DEPTH // 48)
+    @pl.loop(0, DEPTH // 48, unroll=2)
     def _(k):
         rows = pl.ds(pl.multiple_of(k * 48, 16), 48)
         b = b_ref[rows, :]
@@ -279,7 +279,7 @@
             continue
         swap[n].wait()
 
-        @pl.loop(0, 16)
+        @pl.loop(0, 16, unroll=4)
         def _(m):
             rows = pl.ds(pl.multiple_of(m * KEPT, 8), KEPT)
             acc[2 * n, rows, :] += other[n, rows, :128]

time: 125 us -> 125 us (level)
  no operation moved by 1% of the time
where the time goes in v9:
time: 125 us
  Pallas kernels  123 us (98%)
  local copies, waits for them, and re-layouts  1.52 us (1%)
    pallas_call x1, Pallas kernels, ladder(): pl.pallas_call(ladder_kernel, out_shape=jax.ShapeDtypeStruct((ROWS, 192),...  123 us

profile of v9, /device:TPU:32, one launch (start us, length us, event | category | flops | bytes accessed | tf_op | source)
XLA Modules:
  0.0 124.5 jit_solution(2337737587461407886)
XLA Ops:
  0.0 123.0 %shard_map.28 = f32[72,192]{1,0:T(8,128)} custom-call(f32[72,48,384]{2,1,0:T(8,128)} %x_ref.1, f32[576,1536]{1,0:T(8,128)} %bitcast.3), custom_call_target="tpu_custom_call" | custom-call | tf_op jit(solution)/shard_map/pallas_call | solution.py:372
  123.0 1.5 %copy.4 = f32[72,192]{1,0:T(8,128)} copy(f32[72,192]{1,0:T(8,128)} %shard_map.28) | data formatting | bytes 110592
